TPU v7x, 128 devices: a whole 4x4x4 slice. The times are simulated.
128 devices in a mesh: depth: 2 (over core), row: 2 (over x_hi), col: 32 (over z, y, x_lo).
Axes of the slice: x: 4 (x_hi: 2, x_lo: 2; x = x_hi * 2 + x_lo), y: 4, z: 4, core: 2. Of those that a mesh axis runs over, the one named last changes fastest.
Arguments:
- tokens_in: bfloat16 [1024, 6144], P(('depth', 'col'), 'row'), may hold values from -6 to 6
- w_in: bfloat16 [6144, 24576], P('row', ('depth', 'col')), may hold values from -0.078125 to 0.078125
- w_out: bfloat16 [24576, 6144], P(('depth', 'col'), 'row'), may hold values from -0.0390625 to 0.0390625
- grad_output: bfloat16 [1024, 6144], P(('depth', 'col'), 'row'), may hold values from -6 to 6
Outputs:
- output: bfloat16 [1024, 6144], P(('depth', 'col'), 'row')
- grad_input: bfloat16 [1024, 6144], P(('depth', 'col'), 'row')
- grad_w_in: float32 [6144, 24576], P('row', ('depth', 'col'))
- grad_w_out: float32 [24576, 6144], P(('depth', 'col'), 'row')
All inputs are finite; a program needn't handle non-finite values.
Results may differ from a plain program's by a relative error of at most 0.005.
Values may be sent and summed in bfloat16 or wider, within the bound.
A program may use at most 128 MiB of HBM per device.

v0:
```python
import jax
import jax.numpy as jnp
from jax import lax
from jax.sharding import PartitionSpec as P


def gelu_value(hidden):
    inner = 0.7978845608 * (hidden + 0.044715 * hidden * hidden * hidden)
    return 0.5 * hidden * (1.0 + jnp.tanh(inner))


def gelu_slope(hidden):
    inner = 0.7978845608 * (hidden + 0.044715 * hidden * hidden * hidden)
    tangent = jnp.tanh(inner)
    return 0.5 * (1.0 + tangent) + 0.5 * hidden * (1.0 - tangent * tangent) * 0.7978845608 * (
        1.0 + 3.0 * 0.044715 * hidden * hidden
    )


def contract_rows(left, right):
    return lax.dot_general(
        left, right, (((0,), (0,)), ((), ())), preferred_element_type=jnp.float32
    )


def contract_cols(left, right):
    return lax.dot_general(
        left, right, (((1,), (1,)), ((), ())), preferred_element_type=jnp.float32
    )


def per_device(tokens_in, w_in, w_out, grad_output):
    w_in_set, w_out_set = (
        lax.all_gather(w_in, "depth", axis=1, tiled=True),
        lax.all_gather(w_out, "depth", axis=0, tiled=True),
    )
    inputs_slice, cotangent_slice = (
        lax.all_gather(tokens_in, "col", axis=0, tiled=True),
        lax.all_gather(grad_output, "col", axis=0, tiled=True),
    )
    pre_act = lax.psum_scatter(
        jnp.dot(inputs_slice, w_in_set, preferred_element_type=jnp.float32),
        "row",
        scatter_dimension=0,
        tiled=True,
    )
    act_all = lax.all_gather(gelu_value(pre_act).astype(jnp.bfloat16), "row", axis=0, tiled=True)
    output = lax.psum_scatter(
        jnp.dot(act_all, w_out_set, preferred_element_type=jnp.float32),
        "col",
        scatter_dimension=0,
        tiled=True,
    ).astype(jnp.bfloat16)
    d_act = lax.psum_scatter(
        contract_cols(cotangent_slice, w_out_set), "row", scatter_dimension=0, tiled=True
    )
    d_pre_all = lax.all_gather(
        (d_act * gelu_slope(pre_act)).astype(jnp.bfloat16), "row", axis=0, tiled=True
    )
    input_grad = lax.psum_scatter(
        contract_cols(d_pre_all, w_in_set), "col", scatter_dimension=0, tiled=True
    )
    act_owned, dpre_owned = (
        lax.all_to_all(act_all, "depth", split_axis=1, concat_axis=0, tiled=True),
        lax.all_to_all(d_pre_all, "depth", split_axis=1, concat_axis=0, tiled=True),
    )
    inputs_every, cotangent_every = (
        lax.all_gather(inputs_slice, "depth", axis=0, tiled=True),
        lax.all_gather(cotangent_slice, "depth", axis=0, tiled=True),
    )
    grad_w_out = contract_rows(act_owned, cotangent_every)
    grad_w_in = contract_rows(inputs_every, dpre_owned)
    return (output, input_grad.astype(jnp.bfloat16), grad_w_in, grad_w_out)


def solution(mesh):
    placed = (
        P(("depth", "col"), "row"),
        P("row", ("depth", "col")),
        P(("depth", "col"), "row"),
        P(("depth", "col"), "row"),
    )
    return jax.shard_map(
        per_device,
        mesh=mesh,
        in_specs=placed,
        out_specs=(
            P(("depth", "col"), "row"),
            P(("depth", "col"), "row"),
            P("row", ("depth", "col")),
            P(("depth", "col"), "row"),
        ),
        check_vma=False,
    )
```

profile of v0, /device:TPU:0, one launch (start us, length us, event | category | flops | bytes accessed | tf_op | source)
XLA Modules:
  0.0 857.7 jit_solution(9863490890025727098)
XLA Ops:
  10.0 19.3 %all-gather.11.cloned.1.call-done = bf16[768,3072]{1,0:T(8,128)(2,1)} async-done(((bf16[384,3072]{1,0:T(8,128)(2,1)}), bf16[768,3072]{1,0:T(8,128)(2,1)}) %all-gather.11.cloned.1.call-update) | async-done | bytes 4718608 | tf_op jit(solution)/shard_map/all_gather | solution.py:35
  29.3 164.1 %all-gather.13.cloned.1.call-done = bf16[512,3072]{1,0:T(8,128)(2,1)} async-done(((bf16[16,3072]{1,0:T(8,128)(2,1)}), bf16[512,3072]{1,0:T(8,128)(2,1)}) %all-gather.13.cloned.1.call-update) | async-done | bytes 3145744 | tf_op jit(solution)/shard_map/all_gather | solution.py:39
  193.3 7.1 fusion.9
  200.5 11.8 %all-gather.9.cloned.1.call-done = bf16[3072,768]{1,0:T(8,128)(2,1)} async-done(((bf16[3072,384]{1,0:T(8,128)(2,1)}), bf16[3072,768]{1,0:T(8,128)(2,1)}) %all-gather.9.cloned.1.call-update) | async-done | bytes 4718608 | tf_op jit(solution)/shard_map/all_gather | solution.py:34
  212.3 163.9 %all-gather.7.cloned.1.call-done = bf16[512,3072]{1,0:T(8,128)(2,1)} async-done(((bf16[16,3072]{1,0:T(8,128)(2,1)}), bf16[512,3072]{1,0:T(8,128)(2,1)}) %all-gather.7.cloned.1.call-update) | async-done | bytes 3145744 | tf_op jit(solution)/shard_map/all_gather | solution.py:38
  376.2 7.0 fusion.7
  384.8 24.5 %reduce-scatter.9.cloned.1.call-done = f32[256,768]{1,0:T(8,128)} async-done(((f32[512,768]{1,0:T(8,128)}), f32[256,768]{1,0:T(8,128)}) %reduce-scatter.9.cloned.1.call-update) | async-done | bytes 786448 | tf_op jit(solution)/shard_map/reduce_scatter | solution.py:54
  409.4 32.5 %reduce-scatter.5.cloned.1.call-done = f32[256,768]{1,0:T(8,128)} async-done(((f32[512,768]{1,0:T(8,128)}), f32[256,768]{1,0:T(8,128)}) %reduce-scatter.5.cloned.1.call-update) | async-done | bytes 786448 | tf_op jit(solution)/shard_map/reduce_scatter | solution.py:41
  441.8 1.9 fusion.6
  443.8 13.0 %all_gather.26 = bf16[512,768]{1,0:T(8,128)(2,1)S(1)} all-gather(bf16[256,768]{1,0:T(8,128)(2,1)S(1)} %get-tuple-element.13), channel_id=1, replica_groups=mesh['depth'=2,'row'=2,'col'=32] {'row'}, dimensions={0}, use_global_device_ids=true | all-gather | bytes 1179648 | tf_op jit(solution)/shard_map/all_gather | solution.py:47
  456.8 7.7 fusion.8
  464.5 11.8 %all_gather.29 = bf16[512,768]{1,0:T(8,128)(2,1)S(1)} all-gather(bf16[256,768]{1,0:T(8,128)(2,1)S(1)} %get-tuple-element.12), channel_id=1, replica_groups=mesh['depth'=2,'row'=2,'col'=32] {'row'}, dimensions={0}, use_global_device_ids=true | all-gather | bytes 1179648 | tf_op jit(solution)/shard_map/all_gather | solution.py:57
  476.4 7.7 fusion.10
  484.1 1.0 copy.17
  485.1 3.5 all-to-all-start
  488.6 1.0 copy.16
  490.5 3.7 all-to-all-start.1
  494.3 7.6 convolution_bitcast_fusion
  501.9 6.0 copy.11
  507.9 7.7 fusion.11
  515.6 153.2 %reduce-scatter.7.cloned.1.call-done = f32[16,3072]{1,0:T(8,128)} async-done(((f32[512,3072]{1,0:T(8,128)}), f32[16,3072]{1,0:T(8,128)}) %reduce-scatter.7.cloned.1.call-update) | async-done | bytes 196624 | tf_op jit(solution)/shard_map/reduce_scatter | solution.py:48
  668.8 1.6 convert_element_type.13
  670.4 178.9 %reduce-scatter.11.cloned.1.call-done = f32[16,3072]{1,0:T(8,128)} async-done(((f32[512,3072]{1,0:T(8,128)}), f32[16,3072]{1,0:T(8,128)}) %reduce-scatter.11.cloned.1.call-update) | async-done | bytes 196624 | tf_op jit(solution)/shard_map/reduce_scatter | solution.py:60
  849.3 1.6 convert_element_type.15
  (24 shorter events, 5.3 us)
Async XLA Ops:
  7.2 22.1 %all-gather.11.cloned.1.call-start = ((), (), s32[]{:S(2)}) async-start(), calls=%async_computation.9 | async-start | bytes 7077888 | tf_op jit(solution)/shard_map/all_gather | solution.py:35
  7.9 185.4 %all-gather.13.cloned.1.call-start = ((), (), s32[]{:S(2)}) async-start(), calls=%async_computation.11 | async-start | bytes 3244032 | tf_op jit(solution)/shard_map/all_gather | solution.py:39
  8.6 203.6 %all-gather.9.cloned.1.call-start = ((), (), s32[]{:S(2)}) async-start(), calls=%async_computation.7 | async-start | bytes 7077888 | tf_op jit(solution)/shard_map/all_gather | solution.py:34
  9.4 366.8 %all-gather.7.cloned.1.call-start = ((), (), s32[]{:S(2)}) async-start(), calls=%async_computation.6 | async-start | bytes 3244032 | tf_op jit(solution)/shard_map/all_gather | solution.py:38
  10.0 399.4 %reduce-scatter.9.cloned.1.call-start = ((), (), s32[]{:S(2)}) async-start(), calls=%async_computation.12 | async-start | bytes 2359296 | tf_op jit(solution)/shard_map/reduce_scatter | solution.py:54
  200.4 241.4 %reduce-scatter.5.cloned.1.call-start = ((), (), s32[]{:S(2)}) async-start(), calls=%async_computation.8 | async-start | bytes 2359296 | tf_op jit(solution)/shard_map/reduce_scatter | solution.py:41
  383.3 111.0 %all-gather.15.cloned.1.call-start = ((), (), s32[]{:S(2)}) async-start(), calls=%async_computation.14 | async-start | bytes 9437184 | tf_op jit(solution)/shard_map/all_gather | solution.py:68
  384.0 123.9 %all-gather.17.cloned.1.call-start = ((), (), s32[]{:S(2)}) async-start(), calls=%async_computation.15 | async-start | bytes 9437184 | tf_op jit(solution)/shard_map/all_gather | solution.py:69
  384.8 284.1 %reduce-scatter.7.cloned.1.call-start = ((), (), s32[]{:S(2)}) async-start(), calls=%async_computation.10 | async-start | bytes 6488064 | tf_op jit(solution)/shard_map/reduce_scatter | solution.py:48
  464.5 384.8 %reduce-scatter.11.cloned.1.call-start = ((), (), s32[]{:S(2)}) async-start(), calls=%async_computation.13 | async-start | bytes 6488064 | tf_op jit(solution)/shard_map/reduce_scatter | solution.py:60
  485.1 5.5 all-to-all-start
  490.5 17.4 %all-to-all-start.1 = ((bf16[512,2,384]{2,0,1:T(8,128)(2,1)}), bf16[512,2,384]{2,0,1:T(8,128)(2,1)S(1)}, u32[]{:S(2)}, u32[]{:S(2)}) async-start(bf16[512,2,384]{2,0,1:T(8,128)(2,1)} %bitcast.26), calls=%async_computation.5 | async-start | bytes 1572864 | tf_op jit(solution)/shard_map/all_to_all | solution.py:64
Sparse Core Ops, SparseCore 0:
  9.6 19.5 all-gather.10
  30.9 162.3 all-gather.12
  195.0 17.2 all-gather.8
  213.8 162.3 all-gather.6
  379.0 30.3 reduce-scatter.8
  412.3 29.5 reduce-scatter.4
  443.5 18.8 all-gather.14
  464.0 20.7 all-gather.16
  487.3 181.4 reduce-scatter.6
  671.1 178.2 reduce-scatter.10
where the time goes:
time: 858 us
  waiting for transfers between devices  753 us (88%)
  matrix products  44.8 us (5%)
  blocking collectives  24.8 us (3%)
  between operations  14.2 us (2%)
    reduce_scatter x1, waiting for transfers between devices, per_device(): lax.psum_scatter(contract_cols(d_pre_all, w_in_set), 'col', scatter_dimen...  179 us
    all_gather x1, waiting for transfers between devices, per_device(): lax.all_gather(grad_output, 'col', axis=0, tiled=True)  164 us
    all_gather x1, waiting for transfers between devices, per_device(): lax.all_gather(tokens_in, 'col', axis=0, tiled=True)  164 us
    reduce_scatter x1, waiting for transfers between devices, per_device(): lax.psum_scatter(jnp.dot(act_all, w_out_set, preferred_element_type=jnp.f...  153 us
    reduce_scatter x1, waiting for transfers between devices, per_device(): lax.psum_scatter(jnp.dot(inputs_slice, w_in_set, preferred_element_type=j...  32.5 us
    reduce_scatter x1, waiting for transfers between devices, per_device(): lax.psum_scatter(contract_cols(cotangent_slice, w_out_set), 'row', scatte...  24.5 us
    all_gather x1, waiting for transfers between devices, per_device(): lax.all_gather(w_out, 'depth', axis=0, tiled=True)  19.3 us
  transfers between devices with their start and end apart: 12, of which 9 were waited for; matrix products, arithmetic and copies ran while one was open for 7% of the time, Pallas kernels for 0%

commit v1 on v0

v1 whole, which is shorter than its diff:
```python
import functools

import jax
import jax.numpy as jnp
from jax import lax
from jax.experimental import pallas as pl
from jax.experimental.pallas import tpu as pltpu
from jax.sharding import PartitionSpec as P

MESH = pl.DeviceIdType.MESH
BF16, F32 = jnp.bfloat16, jnp.float32
OFFSETS = (0, 1, 3, 2)
N_REMOTE = 128
N_LOCAL = 16


def contract_rows(left, right):
    return lax.dot_general(left, right, (((0,), (0,)), ((), ())), preferred_element_type=F32)


def nn(left, right):
    return jnp.dot(left, right, preferred_element_type=F32)


def nt(left, right):
    return lax.dot_general(left, right, (((1,), (1,)), ((), ())), preferred_element_type=F32)


def kernel(
    tokens, w_in, w_out, cotangent,
    out, gin, tokens_every, cotangent_every, act_every, dpre_every,
    g_tok, g_cot, wi, wo, pre, dact, s_pre, r_pre, s_dact, r_dact, act, dpre,
    q2, r2, mid, s1, r1, acc, u2, v2, fin, s3, r3,
    send, recv, local,
):
    rows, feat = tokens.shape
    hid = w_in.shape[1]
    slab = 4 * rows
    depth, row, col = lax.axis_index("depth"), lax.axis_index("row"), lax.axis_index("col")
    low = lax.rem(col, 2)
    y = lax.rem(lax.div(col, 2), 4)
    z = lax.div(col, 8)

    def at(dy=0, dz=0, lo=None, r=None, d=None):
        c = lax.rem(z + dz, 4) * 8 + lax.rem(y + dy, 4) * 2 + (low if lo is None else lo)
        return (depth if d is None else d, row if r is None else r, c)

    x_partner = at(lo=1 - low)
    row_partner = at(r=1 - row)
    core_partner = at(d=1 - depth)
    along_y = {o: at(dy=o) for o in (1, 2, 3)}
    along_z = {o: at(dz=o) for o in (1, 2, 3)}
    ring1 = (along_z, along_y)
    ring2 = (along_y, along_z)
    own = (y, z)
    sub = (z, y)

    counter, counter_local, sent = [0], [0], []

    def remote(src, dst, device):
        i = counter[0]
        counter[0] += 1
        copy = pltpu.make_async_remote_copy(
            src_ref=src, dst_ref=dst, send_sem=send.at[i], recv_sem=recv.at[i],
            device_id=device, device_id_type=MESH,
        )
        copy.start()
        sent.append(copy)
        return copy

    def here(src, dst):
        i = counter_local[0]
        counter_local[0] += 1
        copy = pltpu.make_async_copy(src, dst, local.at[i])
        copy.start()
        return copy

    def piece(j):
        return pl.ds(pl.multiple_of(j * rows, rows), rows)

    def ring_at(h, o):
        return lax.rem(own[h] + o, 4)

    my_i = y + low * (z - y)
    my_j = z + low * (y - z)
    own_copies = [
        here(tokens, g_tok.at[low, my_i, piece(my_j)]),
        here(cotangent, g_cot.at[low, my_i, piece(my_j)]),
    ]
    weight_copies = [
        here(w_in, wi.at[:, pl.ds(0, hid)]),
        here(w_out, wo.at[pl.ds(0, hid)]),
    ]

    barrier = pltpu.get_barrier_semaphore()
    friends = [x_partner, row_partner, core_partner] + list(along_y.values()) + list(along_z.values())
    for friend in friends:
        pl.semaphore_signal(barrier, inc=1, device_id=friend, device_id_type=MESH)
    pl.semaphore_wait(barrier, len(friends))

    gathered = (g_tok, g_cot)
    g0 = [
        remote(src, g.at[low, my_i, piece(my_j)], x_partner)
        for src, g in ((tokens, g_tok), (cotangent, g_cot))
    ]
    weight_in = remote(w_in, wi.at[:, pl.ds(hid, hid)], core_partner)
    weight_out = remote(w_out, wo.at[pl.ds(hid, hid)], core_partner)

    def gather_one(g):
        copies = []
        for h in range(2):
            block = g.at[h, own[h], piece(sub[h])]
            copies += [remote(block, block, ring1[h][o]) for o in (1, 3, 2)]
        return copies

    def half(k):
        return pl.ds(k * 2 * rows, 2 * rows)

    def gather_two(g):
        first, second = [], []
        for h in range(2):
            for o, order in ((1, (0, 1)), (3, (1, 0))):
                part = [g.at[h, own[h], half(k)] for k in order]
                first.append(remote(part[0], part[0], ring2[h][o]))
        for h in range(2):
            for o, order in ((1, (0, 1)), (3, (1, 0))):
                part = g.at[h, own[h], half(order[1])]
                second.append(remote(part, part, ring2[h][o]))
        return first, second

    def gather_three(g):
        copies = []
        for h in range(2):
            left = g.at[h, ring_at(h, 3), half(0)]
            copies.append(remote(left, left, ring2[h][1]))
            right = g.at[h, ring_at(h, 1), half(1)]
            copies.append(remote(right, right, ring2[h][3]))
        return copies

    def arrived(copies):
        for copy in copies:
            copy.wait_recv()

    g1 = []
    for k in range(2):
        own_copies[k].wait()
        g0[k].wait_recv()
        g1.append(gather_one(gathered[k]))
    arrived(g1[0])
    x2 = gather_two(g_tok)

    tile = 256
    n_hid = 2 * hid // tile

    def rows_of(g, o):
        return jnp.concatenate([g[h, ring_at(h, o)] for h in range(2)], axis=0)

    def pre_step(s):
        chunk = rows_of(g_tok, OFFSETS[s])

        def body(t, _):
            cols = pl.ds(pl.multiple_of(t * tile, tile), tile)
            value = nn(chunk, wi[:, cols])
            pre[s, :, cols] = value
            s_pre[s, :, cols] = value.astype(BF16)
            return 0

        lax.fori_loop(0, n_hid, body, 0)
        return remote(s_pre.at[s], r_pre.at[s], row_partner)

    def dact_step(s):
        chunk = rows_of(g_cot, OFFSETS[s])

        def body(t, _):
            cols = pl.ds(pl.multiple_of(t * tile, tile), tile)
            value = nt(chunk, wo[cols, :])
            dact[s, :, cols] = value
            s_dact[s, :, cols] = value.astype(BF16)
            return 0

        lax.fori_loop(0, n_hid, body, 0)
        return remote(s_dact.at[s], r_dact.at[s], row_partner)

    def act_step(s, copy):
        copy.wait_recv()
        for h in range(2):
            i = ring_at(h, OFFSETS[s])

            def body(t, _):
                r_in = pl.ds(pl.multiple_of(h * slab + t * 16, 16), 16)
                r_out = pl.ds(pl.multiple_of(t * 16, 16), 16)
                hidden = pre[s, r_in, :] + r_pre[s, r_in, :].astype(F32)
                square = hidden * hidden
                inner = 0.7978845608 * (hidden + 0.044715 * square * hidden)
                tangent = jnp.tanh(inner)
                act[h, i, r_out, :] = (0.5 * hidden * (1.0 + tangent)).astype(BF16)
                pre[s, r_in, :] = 0.5 * (1.0 + tangent) + 0.5 * hidden * (
                    1.0 - tangent * tangent
                ) * 0.7978845608 * (1.0 + 3.0 * 0.044715 * square)
                return 0

            lax.fori_loop(0, slab // 16, body, 0)

    def dpre_step(s, copy):
        copy.wait_recv()
        for h in range(2):
            i = ring_at(h, OFFSETS[s])

            def body(t, _):
                r_in = pl.ds(pl.multiple_of(h * slab + t * 16, 16), 16)
                r_out = pl.ds(pl.multiple_of(t * 16, 16), 16)
                total = dact[s, r_in, :] + r_dact[s, r_in, :].astype(F32)
                dpre[h, i, r_out, :] = (total * pre[s, r_in, :]).astype(BF16)
                return 0

            lax.fori_loop(0, slab // 16, body, 0)

    wide = 512
    n_wide = feat // wide
    low_rows, high_rows = slice(0, 2 * rows), slice(2 * rows, 4 * rows)

    def project(k, s):
        chunk = rows_of((act, dpre)[k], OFFSETS[s])
        o = OFFSETS[s]

        def body(t, _):
            cols = pl.ds(pl.multiple_of(t * wide, wide), wide)
            value = nn(chunk, wo[:, cols]) if k == 0 else nt(chunk, wi[cols, :])
            for h in range(2):
                part = value[h * slab:(h + 1) * slab]
                if o == 2:
                    q2[k, h, :, cols] = part.astype(BF16)
                elif o == 1:
                    s1[k, h, 0, high_rows, cols] = part[high_rows].astype(BF16)
                    mid[k, h, 0, :, cols] = part[low_rows]
                elif o == 3:
                    s1[k, h, 1, low_rows, cols] = part[low_rows].astype(BF16)
                    mid[k, h, 1, :, cols] = part[high_rows]
                else:
                    acc[k, h, :, cols] = part
            return 0

        lax.fori_loop(0, n_wide, body, 0)

    def scatter_far(k):
        copies = []
        for h in range(2):
            copies.append(remote(q2.at[k, h, low_rows], r2.at[k, h, 0], ring2[h][1]))
            copies.append(remote(q2.at[k, h, high_rows], r2.at[k, h, 1], ring2[h][3]))
        return copies

    def scatter_near(k, side):
        part = (high_rows, low_rows)[side]
        return [
            remote(s1.at[k, h, side, part], r1.at[k, h, side, part], ring2[h][(1, 3)[side]])
            for h in range(2)
        ]

    def scatter_merge(k, far):
        copies = []
        for h in range(2):
            for side in range(2):
                far[2 * h + side].wait_recv()
                base = side * 2 * rows

                def body(t, _):
                    r_in = pl.ds(pl.multiple_of(t * 16, 16), 16)
                    r_out = pl.ds(pl.multiple_of(base + t * 16, 16), 16)
                    total = mid[k, h, side, r_in, :] + r2[k, h, side, r_in, :].astype(F32)
                    s1[k, h, side, r_out, :] = total.astype(BF16)
                    return 0

                lax.fori_loop(0, 2 * rows // 16, body, 0)
                part = (low_rows, high_rows)[side]
                copies.append(
                    remote(s1.at[k, h, side, part], r1.at[k, h, side, part], ring2[h][(1, 3)[side]])
                )
        return copies

    def scatter_two(k, near, merged):
        arrived(near)
        arrived(merged)
        copies = []
        for h in range(2):
            for slot, o in enumerate((1, 3, 2)):
                r_in = piece(lax.rem(sub[h] + o, 4))
                total = acc[k, h, r_in, :] + r1[k, h, 0, r_in, :].astype(F32)
                u2[k, h, slot] = (total + r1[k, h, 1, r_in, :].astype(F32)).astype(BF16)
                copies.append(remote(u2.at[k, h, slot], v2.at[k, h, slot], ring1[h][o]))
        return copies

    def scatter_three(k, copies):
        arrived(copies)
        for h in range(2):
            r_in = piece(sub[h])
            total = acc[k, h, r_in, :] + r1[k, h, 0, r_in, :].astype(F32)
            total += r1[k, h, 1, r_in, :].astype(F32)
            for slot in range(3):
                total += v2[k, h, slot].astype(F32)
            fin[k, h] = total
        s3[k] = fin[k, 1 - low].astype(BF16)
        return remote(s3.at[k], r3.at[k], x_partner)

    def finish(k, copy):
        copy.wait_recv()
        (out, gin)[k][...] = (fin[k, low] + r3[k].astype(F32)).astype(BF16)

    weight_copies[0].wait()
    weight_in.wait_recv()
    p = [pre_step(0)]
    arrived(x2[0])
    x3 = gather_three(g_tok)
    arrived(g1[1])
    c2 = gather_two(g_cot)
    arrived(x2[1])
    p.append(pre_step(1))
    p.append(pre_step(2))
    arrived(x3)
    p.append(pre_step(3))
    every = [here(g_tok, tokens_every.at[0]), remote(g_tok, tokens_every.at[1], core_partner)]
    weight_copies[1].wait()
    weight_out.wait_recv()
    q = [dact_step(0)]
    act_step(0, p[0])
    arrived(c2[0])
    c3 = gather_three(g_cot)
    act_step(1, p[1])
    act_step(2, p[2])
    act_step(3, p[3])
    project(0, 3)
    far0 = scatter_far(0)
    project(0, 1)
    near0 = scatter_near(0, 0)
    project(0, 2)
    near0 += scatter_near(0, 1)
    arrived(c2[1])
    q.append(dact_step(1))
    q.append(dact_step(2))
    arrived(c3)
    q.append(dact_step(3))
    merged0 = scatter_merge(0, far0)
    project(0, 0)
    every += [here(g_cot, cotangent_every.at[0]), remote(g_cot, cotangent_every.at[1], core_partner)]
    mine, other = pl.ds(0, hid), pl.ds(hid, hid)
    every += [
        here(act.at[:, :, :, mine], act_every.at[0]),
        remote(act.at[:, :, :, other], act_every.at[1], core_partner),
    ]
    dpre_step(3, q[3])
    project(1, 3)
    far1 = scatter_far(1)
    dpre_step(1, q[1])
    project(1, 1)
    near1 = scatter_near(1, 0)
    dpre_step(2, q[2])
    project(1, 2)
    near1 += scatter_near(1, 1)
    two0 = scatter_two(0, near0, merged0)
    dpre_step(0, q[0])
    project(1, 0)
    every += [
        here(dpre.at[:, :, :, mine], dpre_every.at[0]),
        remote(dpre.at[:, :, :, other], dpre_every.at[1], core_partner),
    ]
    merged1 = scatter_merge(1, far1)
    three0 = scatter_three(0, two0)
    finish(0, three0)
    two1 = scatter_two(1, near1, merged1)
    three1 = scatter_three(1, two1)
    finish(1, three1)
    for i in range(0, len(every), 2):
        every[i].wait()
        every[i + 1].wait_recv()
    for copy in sent:
        copy.wait_send()


def exchange(tokens_in, w_in, w_out, grad_output):
    rows, feat = tokens_in.shape
    hid = w_in.shape[1]
    slab = 4 * rows
    vmem, hbm = pl.BlockSpec(memory_space=pltpu.VMEM), pl.BlockSpec(memory_space=pl.ANY)
    shape = jax.ShapeDtypeStruct
    scratch = [
        ((2, 4, slab, feat), BF16),
        ((2, 4, slab, feat), BF16),
        ((feat, 2 * hid), BF16),
        ((2 * hid, feat), BF16),
        ((4, 2 * slab, 2 * hid), F32),
        ((4, 2 * slab, 2 * hid), F32),
        ((4, 2 * slab, 2 * hid), BF16),
        ((4, 2 * slab, 2 * hid), BF16),
        ((4, 2 * slab, 2 * hid), BF16),
        ((4, 2 * slab, 2 * hid), BF16),
        ((2, 4, slab, 2 * hid), BF16),
        ((2, 4, slab, 2 * hid), BF16),
        ((2, 2, slab, feat), BF16),
        ((2, 2, 2, 2 * rows, feat), BF16),
        ((2, 2, 2, 2 * rows, feat), F32),
        ((2, 2, 2, slab, feat), BF16),
        ((2, 2, 2, slab, feat), BF16),
        ((2, 2, slab, feat), F32),
        ((2, 2, 3, rows, feat), BF16),
        ((2, 2, 3, rows, feat), BF16),
        ((2, 2, rows, feat), F32),
        ((2, rows, feat), BF16),
        ((2, rows, feat), BF16),
    ]
    return pl.pallas_call(
        kernel,
        out_shape=[
            shape((rows, feat), BF16),
            shape((rows, feat), BF16),
            shape((2, 2, 4, slab, feat), BF16),
            shape((2, 2, 4, slab, feat), BF16),
            shape((2, 2, 4, slab, hid), BF16),
            shape((2, 2, 4, slab, hid), BF16),
        ],
        in_specs=[hbm] * 4,
        out_specs=[vmem] * 2 + [hbm] * 4,
        scratch_shapes=[pltpu.VMEM(*s) for s in scratch] + [
            pltpu.SemaphoreType.DMA((N_REMOTE,)),
            pltpu.SemaphoreType.DMA((N_REMOTE,)),
            pltpu.SemaphoreType.DMA((N_LOCAL,)),
        ],
        compiler_params=pltpu.CompilerParams(
            collective_id=0, has_side_effects=True, vmem_limit_bytes=60 * 2**20
        ),
        name="exchange",
    )(tokens_in, w_in, w_out, grad_output)


def per_device(tokens_in, w_in, w_out, grad_output):
    feat, hid = w_in.shape
    output, grad_input, tokens_every, cotangent_every, act_owned, dpre_owned = exchange(
        tokens_in, w_in, w_out, grad_output
    )
    grad_w_out = contract_rows(act_owned.reshape(-1, hid), cotangent_every.reshape(-1, feat))
    grad_w_in = contract_rows(tokens_every.reshape(-1, feat), dpre_owned.reshape(-1, hid))
    return (output, grad_input, grad_w_in, grad_w_out)


def solution(mesh):
    placed = (
        P(("depth", "col"), "row"),
        P("row", ("depth", "col")),
        P(("depth", "col"), "row"),
        P(("depth", "col"), "row"),
    )
    return jax.shard_map(
        per_device,
        mesh=mesh,
        in_specs=placed,
        out_specs=(
            P(("depth", "col"), "row"),
            P(("depth", "col"), "row"),
            P("row", ("depth", "col")),
            P(("depth", "col"), "row"),
        ),
        check_vma=False,
    )
```

time: 858 us -> 113 us (0.13)
  waiting for transfers between devices: 753 us -> 0 us
  Pallas kernels: 0 us -> 97.4 us
  matrix products: 44.8 us -> 13 us
  blocking collectives: 24.8 us -> 0 us
  between operations: 14.2 us -> 0.67 us
    reduce_scatter x4 -> x0, waiting for transfers between devices: 389 us -> none  [the longest x1 179 us: per_device(): lax.psum_scatter(contract_cols(d_pre_all, w_in_set), 'col', scatter_dimen...]
    all_gather x6 -> x0, waiting for transfers between devices: 359 us -> none  [the longest x1 164 us: per_device(): lax.all_gather(grad_output, 'col', axis=0, tiled=True)]
    pallas_call x0 -> x1, Pallas kernels: none -> 97.4 us  [exchange(): pl.pallas_call(kernel, out_shape=[shape((rows, feat), BF16), shape((rows,...]
    dot_general x4 -> x0, matrix products: 29.5 us -> none  [the longest x2 14.8 us: contract_cols(): lax.dot_general(left, right, (((1,), (1,)), ((), ())), preferred_element_...]
    all_gather x2 -> x0, blocking collectives: 24.8 us -> none  [the longest x1 13 us: per_device(): lax.all_gather(gelu_value(pre_act).astype(jnp.bfloat16), 'row', axis=0, t...]
  transfers between devices with their start and end apart: 12 -> 0, of which waited for: 9 -> 0; matrix products, arithmetic and copies ran while one was open for 7% -> 0% of each run, Pallas kernels for 0% -> 0%
where the time goes in v1:
time: 113 us; the launch traced here: 112 us
  Pallas kernels  97.4 us (86%)
  matrix products  13 us (12%)
  local copies, waits for them, and re-layouts  1.3 us (1%)
    pallas_call x1, Pallas kernels, exchange(): pl.pallas_call(kernel, out_shape=[shape((rows, feat), BF16), shape((rows,...  97.4 us
    dot_general x2, matrix products, contract_rows(): lax.dot_general(left, right, (((0,), (0,)), ((), ())), preferred_element_...  13 us

profile of v1, /device:TPU:0, one launch (start us, length us, event | category | flops | bytes accessed | tf_op | source)
XLA Modules:
  0.0 112.4 jit_solution(11713376286110436857)
XLA Ops:
  0.6 97.4 %exchange.1 = (bf16[16,3072]{1,0:T(8,128)(2,1)}, bf16[16,3072]{1,0:T(8,128)(2,1)}, bf16[2,2,4,64,3072]{4,3,2,1,0:T(8,128)(2,1)}, bf16[2,2,4,64,3072]{4,3,2,1,0:T...) custom-call(bf16[16,3072]{1,0:T(8,128)(2,1)} %tokens.1, bf16[3072,384]{1,0:T(8,128)(2,1)} %w_in.1, ...), custom_call_target="tpu_custom_call" | custom-call | tf_op jit(solution)/shard_map/exchange/pallas_call | solution.py:409
  98.0 0.0 copy-start.2
  98.1 0.0 copy-start.3
  98.1 8.8 %convolution_bitcast_fusion.1 = f32[3072,384]{1,0:T(8,128)} fusion(bf16[2,2,4,64,3072]{4,3,2,1,0:T(8,128)(2,1)} %get-tuple-element.12, bf16[2,2,4,64,384]{4,3,2,1,0:T(8,128)(2,1)} %get-tuple-element.13), kind=kOutput, calls=%fused_computation.1 | convolution fusion | flops 2415919104 | bytes 11796480 | tf_op jit(solution)/shard_map/dot_general | solution.py:18
  106.8 0.0 copy-done.2
  106.8 0.0 copy-done.3
  106.8 0.0 copy-start.1
  106.8 0.0 copy-start
  106.8 4.3 %convolution_bitcast_fusion = f32[384,3072]{1,0:T(8,128)} fusion(bf16[2,2,4,64,384]{4,3,2,1,0:T(8,128)(2,1)S(1)} %copy-done.3, bf16[2,2,4,64,3072]{4,3,2,1,0:T(8,128)(2,1)S(1)} %copy-done.2), kind=kOutput, calls=%fused_computation | convolution fusion | flops 2415919104 | bytes 11796480 | tf_op jit(solution)/shard_map/dot_general | solution.py:18
  111.1 0.0 copy-done.1
  111.1 0.6 copy.12
  111.8 0.0 copy-done
  111.8 0.6 copy.13
Async XLA Ops:
  98.0 8.8 %copy-start.2 = (bf16[2,2,4,64,3072]{4,3,2,1,0:T(8,128)(2,1)S(1)}, bf16[2,2,4,64,3072]{4,3,2,1,0:T(8,128)(2,1)}, u32[]{:S(2)}) copy-start(bf16[2,2,4,64,3072]{4,3,2,1,0:T(8,128)(2,1)} %get-tuple-element.15) | copy-start | bytes 18874372
  98.1 8.8 %copy-start.3 = (bf16[2,2,4,64,384]{4,3,2,1,0:T(8,128)(2,1)S(1)}, bf16[2,2,4,64,384]{4,3,2,1,0:T(8,128)(2,1)}, u32[]{:S(2)}) copy-start(bf16[2,2,4,64,384]{4,3,2,1,0:T(8,128)(2,1)} %get-tuple-element.14) | copy-start | bytes 2359300
  106.8 4.3 %copy-start.1 = (bf16[16,3072]{1,0:T(8,128)(2,1)S(1)}, bf16[16,3072]{1,0:T(8,128)(2,1)}, u32[]{:S(2)}) copy-start(bf16[16,3072]{1,0:T(8,128)(2,1)} %get-tuple-element.20) | copy-start | bytes 294916
  106.8 4.9 %copy-start = (bf16[16,3072]{1,0:T(8,128)(2,1)S(1)}, bf16[16,3072]{1,0:T(8,128)(2,1)}, u32[]{:S(2)}) copy-start(bf16[16,3072]{1,0:T(8,128)(2,1)} %get-tuple-element.21) | copy-start | bytes 294916

commit v2 on v1

--- a/solution.py
+++ b/solution.py
@@ -28,8 +28,8 @@
 
 def kernel(
     tokens, w_in, w_out, cotangent,
-    out, gin, tokens_every, cotangent_every, act_every, dpre_every,
-    g_tok, g_cot, wi, wo, pre, dact, s_pre, r_pre, s_dact, r_dact, act, dpre,
+    out, gin, grad_in, grad_out,
+    g_tok, g_cot, e_tok, e_cot, e_act, e_dpre, act_t, wi, wo, pre, dact, s_pre, r_pre, s_dact, r_dact, act, dpre,
     q2, r2, mid, s1, r1, acc, u2, v2, fin, s3, r3,
     send, recv, local,
 ):
@@ -305,6 +305,35 @@
         copy.wait_recv()
         (out, gin)[k][...] = (fin[k, low] + r3[k].astype(F32)).astype(BF16)
 
+    mine, other = pl.ds(0, hid), pl.ds(hid, hid)
+    tokens_all = 8 * slab
+
+    def flat(value):
+        return value.reshape(tokens_all, value.shape[-1])
+
+    def turn_act():
+        act_t[0] = jnp.transpose(flat(act[:, :, :, mine]))
+        act_t[1] = jnp.transpose(flat(e_act[...]))
+
+    def grad_out_part(start, stop):
+        def body(t, _):
+            cols = pl.ds(pl.multiple_of(t * tile, tile), tile)
+            value = nn(act_t[0], flat(g_cot[:, :, :, cols]))
+            grad_out[:, cols] = value + nn(act_t[1], flat(e_cot[:, :, :, cols]))
+            return 0
+
+        lax.fori_loop(start, stop, body, 0)
+
+    def grad_in_part(start, stop):
+        def body(t, _):
+            cols = pl.ds(pl.multiple_of(t * tile, tile), tile)
+            value = contract_rows(flat(g_tok[:, :, :, cols]), flat(dpre[:, :, :, mine]))
+            value += contract_rows(flat(e_tok[:, :, :, cols]), flat(e_dpre[...]))
+            grad_in[cols, :] = value
+            return 0
+
+        lax.fori_loop(start, stop, body, 0)
+
     weight_copies[0].wait()
     weight_in.wait_recv()
     p = [pre_step(0)]
@@ -317,7 +346,7 @@
     p.append(pre_step(2))
     arrived(x3)
     p.append(pre_step(3))
-    every = [here(g_tok, tokens_every.at[0]), remote(g_tok, tokens_every.at[1], core_partner)]
+    every_tok = remote(g_tok, e_tok, core_partner)
     weight_copies[1].wait()
     weight_out.wait_recv()
     q = [dact_step(0)]
@@ -333,19 +362,14 @@
     near0 = scatter_near(0, 0)
     project(0, 2)
     near0 += scatter_near(0, 1)
+    every_act = remote(act.at[:, :, :, other], e_act, core_partner)
     arrived(c2[1])
-    q.append(dact_step(1))
-    q.append(dact_step(2))
     arrived(c3)
-    q.append(dact_step(3))
+    q += [None, None, dact_step(3)]
+    q[1] = dact_step(1)
+    q[2] = dact_step(2)
     merged0 = scatter_merge(0, far0)
-    project(0, 0)
-    every += [here(g_cot, cotangent_every.at[0]), remote(g_cot, cotangent_every.at[1], core_partner)]
-    mine, other = pl.ds(0, hid), pl.ds(hid, hid)
-    every += [
-        here(act.at[:, :, :, mine], act_every.at[0]),
-        remote(act.at[:, :, :, other], act_every.at[1], core_partner),
-    ]
+    every_cot = remote(g_cot, e_cot, core_partner)
     dpre_step(3, q[3])
     project(1, 3)
     far1 = scatter_far(1)
@@ -355,22 +379,25 @@
     dpre_step(2, q[2])
     project(1, 2)
     near1 += scatter_near(1, 1)
+    project(0, 0)
     two0 = scatter_two(0, near0, merged0)
     dpre_step(0, q[0])
+    every_dpre = remote(dpre.at[:, :, :, other], e_dpre, core_partner)
+    merged1 = scatter_merge(1, far1)
     project(1, 0)
-    every += [
-        here(dpre.at[:, :, :, mine], dpre_every.at[0]),
-        remote(dpre.at[:, :, :, other], dpre_every.at[1], core_partner),
-    ]
-    merged1 = scatter_merge(1, far1)
+    every_act.wait_recv()
+    turn_act()
     three0 = scatter_three(0, two0)
+    every_cot.wait_recv()
+    grad_out_part(0, feat // tile)
     finish(0, three0)
     two1 = scatter_two(1, near1, merged1)
+    every_tok.wait_recv()
+    every_dpre.wait_recv()
+    grad_in_part(0, feat // tile // 2)
     three1 = scatter_three(1, two1)
+    grad_in_part(feat // tile // 2, feat // tile)
     finish(1, three1)
-    for i in range(0, len(every), 2):
-        every[i].wait()
-        every[i + 1].wait_recv()
     for copy in sent:
         copy.wait_send()
 
@@ -380,10 +407,14 @@
     hid = w_in.shape[1]
     slab = 4 * rows
     vmem, hbm = pl.BlockSpec(memory_space=pltpu.VMEM), pl.BlockSpec(memory_space=pl.ANY)
-    shape = jax.ShapeDtypeStruct
     scratch = [
         ((2, 4, slab, feat), BF16),
         ((2, 4, slab, feat), BF16),
+        ((2, 4, slab, feat), BF16),
+        ((2, 4, slab, feat), BF16),
+        ((2, 4, slab, hid), BF16),
+        ((2, 4, slab, hid), BF16),
+        ((2, hid, 8 * slab), BF16),
         ((feat, 2 * hid), BF16),
         ((2 * hid, feat), BF16),
         ((4, 2 * slab, 2 * hid), F32),
@@ -409,35 +440,50 @@
     return pl.pallas_call(
         kernel,
         out_shape=[
-            shape((rows, feat), BF16),
-            shape((rows, feat), BF16),
-            shape((2, 2, 4, slab, feat), BF16),
-            shape((2, 2, 4, slab, feat), BF16),
-            shape((2, 2, 4, slab, hid), BF16),
-            shape((2, 2, 4, slab, hid), BF16),
+            pltpu.VMEM((rows, feat), BF16),
+            pltpu.VMEM((rows, feat), BF16),
+            pltpu.VMEM((feat, hid), F32),
+            pltpu.VMEM((hid, feat), F32),
         ],
         in_specs=[hbm] * 4,
-        out_specs=[vmem] * 2 + [hbm] * 4,
+        out_specs=[vmem] * 4,
         scratch_shapes=[pltpu.VMEM(*s) for s in scratch] + [
             pltpu.SemaphoreType.DMA((N_REMOTE,)),
             pltpu.SemaphoreType.DMA((N_REMOTE,)),
             pltpu.SemaphoreType.DMA((N_LOCAL,)),
         ],
         compiler_params=pltpu.CompilerParams(
-            collective_id=0, has_side_effects=True, vmem_limit_bytes=60 * 2**20
+            collective_id=0, has_side_effects=True, vmem_limit_bytes=52 * 2**20
         ),
         name="exchange",
     )(tokens_in, w_in, w_out, grad_output)
 
 
-def per_device(tokens_in, w_in, w_out, grad_output):
-    feat, hid = w_in.shape
-    output, grad_input, tokens_every, cotangent_every, act_owned, dpre_owned = exchange(
-        tokens_in, w_in, w_out, grad_output
-    )
-    grad_w_out = contract_rows(act_owned.reshape(-1, hid), cotangent_every.reshape(-1, feat))
-    grad_w_in = contract_rows(tokens_every.reshape(-1, feat), dpre_owned.reshape(-1, hid))
-    return (output, grad_input, grad_w_in, grad_w_out)
+def drain_kernel(*refs):
+    n = len(refs) // 2
+    copies = [pltpu.make_async_copy(refs[i], refs[n + i], refs[-1].at[i]) for i in range(n)]
+    for copy in copies:
+        copy.start()
+    for copy in copies:
+        copy.wait()
+
+
+def drain(arrays):
+    arrays = [pltpu.with_memory_space_constraint(a, pltpu.VMEM) for a in arrays]
+    anywhere = [pl.BlockSpec(memory_space=pl.ANY)] * len(arrays)
+    return pl.pallas_call(
+        drain_kernel,
+        out_shape=[pltpu.HBM(a.shape, a.dtype) for a in arrays],
+        in_specs=anywhere,
+        out_specs=anywhere,
+        scratch_shapes=[pltpu.SemaphoreType.DMA((len(arrays),))],
+        compiler_params=pltpu.CompilerParams(vmem_limit_bytes=2**20),
+        name="drain",
+    )(*arrays)
+
+
+def per_device(*arrays):
+    return tuple(drain(exchange(*arrays)))
 
 
 def solution(mesh):

time: 113 us -> 96.5 us (0.85)
  matrix products: 13 us -> 0 us
  Pallas kernels: 97.4 us -> 95.5 us
  local copies, waits for them, and re-layouts: 1.3 us -> 0 us
    dot_general x2 -> x0, matrix products: 13 us -> none  [contract_rows(): lax.dot_general(left, right, (((0,), (0,)), ((), ())), preferred_element_...]
    pallas_call x1 -> x2, Pallas kernels: 97.4 us -> 95.5 us  [the longest x1 91.7 us: exchange(): pl.pallas_call(kernel, out_shape=[pltpu.VMEM((rows, feat), BF16), pltpu.V...]
    unnamed x10 -> x0, local copies, waits for them, and re-layouts: 1.3 us -> none
where the time goes in v2:
time: 96.5 us; the launch traced here: 96.2 us
  Pallas kernels  95.5 us (99%)
    pallas_call x1, Pallas kernels, exchange(): pl.pallas_call(kernel, out_shape=[pltpu.VMEM((rows, feat), BF16), pltpu.V...  91.7 us
    pallas_call x1, Pallas kernels, drain(): pl.pallas_call(drain_kernel, out_shape=[pltpu.HBM(a.shape, a.dtype) for a...  3.84 us

profile of v2, /device:TPU:0, one launch (start us, length us, event | category | flops | bytes accessed | tf_op | source)
XLA Modules:
  0.0 96.2 jit_solution(7420116360559153304)
XLA Ops:
  0.6 91.7 %exchange.1 = (bf16[16,3072]{1,0:T(8,128)(2,1)S(1)}, bf16[16,3072]{1,0:T(8,128)(2,1)S(1)}, f32[3072,384]{1,0:T(8,128)S(1)}, f32[384,3072]{1,0:T(8,128)S(1)}) custom-call(bf16[16,3072]{1,0:T(8,128)(2,1)} %tokens.1, bf16[3072,384]{1,0:T(8,128)(2,1)} %w_in.1, bf16[384,3072]{1,0:T(8,128)(2,1)} %w_out.1, bf16[16,3072]{1,0:T(8,128)(2,1)} %cotangent.1), custom_call_target="tpu_custom_call" | custom-call | tf_op jit(solution)/shard_map/exchange/pallas_call | solution.py:440
  92.3 3.8 %drain.1 = (bf16[16,3072]{1,0:T(8,128)(2,1)}, bf16[16,3072]{1,0:T(8,128)(2,1)}, f32[3072,384]{1,0:T(8,128)}, f32[384,3072]{1,0:T(8,128)}) custom-call(bf16[16,3072]{1,0:T(8,128)(2,1)S(1)} %get-tuple-element.8.refs_0_, bf16[16,3072]{1,0:T(8,128)(2,1)S(1)} %get-tuple-element.9.refs_1_, f32[3072,384]{1,0:T(8,128)S(1)} %get-tuple-element.10.refs_2_, ...), custom_call_target="tpu_custom_call" | custom-call | tf_op jit(solution)/shard_map/drain/pallas_call | solution.py:474

commit v3 on v2

--- a/solution.py
+++ b/solution.py
@@ -10,7 +10,7 @@
 MESH = pl.DeviceIdType.MESH
 BF16, F32 = jnp.bfloat16, jnp.float32
 OFFSETS = (0, 1, 3, 2)
-N_REMOTE = 128
+N_REMOTE = 160
 N_LOCAL = 16
 
 
@@ -81,12 +81,8 @@
     def ring_at(h, o):
         return lax.rem(own[h] + o, 4)
 
-    my_i = y + low * (z - y)
-    my_j = z + low * (y - z)
-    own_copies = [
-        here(tokens, g_tok.at[low, my_i, piece(my_j)]),
-        here(cotangent, g_cot.at[low, my_i, piece(my_j)]),
-    ]
+    my_block = (low, y + low * (z - y), piece(z + low * (y - z)))
+    own_copies = [here(tokens, g_tok.at[my_block]), here(cotangent, g_cot.at[my_block])]
     weight_copies = [
         here(w_in, wi.at[:, pl.ds(0, hid)]),
         here(w_out, wo.at[pl.ds(0, hid)]),
@@ -98,56 +94,81 @@
         pl.semaphore_signal(barrier, inc=1, device_id=friend, device_id_type=MESH)
     pl.semaphore_wait(barrier, len(friends))
 
-    gathered = (g_tok, g_cot)
-    g0 = [
-        remote(src, g.at[low, my_i, piece(my_j)], x_partner)
-        for src, g in ((tokens, g_tok), (cotangent, g_cot))
-    ]
-    weight_in = remote(w_in, wi.at[:, pl.ds(hid, hid)], core_partner)
-    weight_out = remote(w_out, wo.at[pl.ds(hid, hid)], core_partner)
-
-    def gather_one(g):
-        copies = []
-        for h in range(2):
-            block = g.at[h, own[h], piece(sub[h])]
-            copies += [remote(block, block, ring1[h][o]) for o in (1, 3, 2)]
-        return copies
-
-    def half(k):
-        return pl.ds(k * 2 * rows, 2 * rows)
-
-    def gather_two(g):
-        first, second = [], []
-        for h in range(2):
-            for o, order in ((1, (0, 1)), (3, (1, 0))):
-                part = [g.at[h, own[h], half(k)] for k in order]
-                first.append(remote(part[0], part[0], ring2[h][o]))
-        for h in range(2):
-            for o, order in ((1, (0, 1)), (3, (1, 0))):
-                part = g.at[h, own[h], half(order[1])]
-                second.append(remote(part, part, ring2[h][o]))
-        return first, second
-
-    def gather_three(g):
-        copies = []
-        for h in range(2):
-            left = g.at[h, ring_at(h, 3), half(0)]
-            copies.append(remote(left, left, ring2[h][1]))
-            right = g.at[h, ring_at(h, 1), half(1)]
-            copies.append(remote(right, right, ring2[h][3]))
-        return copies
-
     def arrived(copies):
         for copy in copies:
             copy.wait_recv()
 
-    g1 = []
-    for k in range(2):
+    def half_of(kind):
+        return low if kind == 0 else 1 - low
+
+    def place(kind, di, j):
+        h = half_of(kind)
+        i0, j0 = y + h * (z - y), z + h * (y - z)
+        return h, lax.rem(i0 + di, 4), piece(lax.rem(j0 + j, 4))
+
+    def to_ring1(kind, o):
+        h = half_of(kind)
+        return at(dy=o * h, dz=o * (1 - h))
+
+    def to_ring2(kind, o):
+        h = half_of(kind)
+        return at(dy=o * (1 - h), dz=o * h)
+
+    def gather_ring1(g, kind, src=None):
+        block = g.at[place(kind, 0, 0)]
+        return {o: remote(block if src is None else src, block, to_ring1(kind, o)) for o in (1, 3, 2)}
+
+    def gather_ring2(g, kind, j, src=None):
+        block = g.at[place(kind, 0, j)]
+        return {o: remote(block if src is None else src, block, to_ring2(kind, o)) for o in (1, 3)}
+
+    def gather_forward(g, kind, j, o):
+        block = g.at[place(kind, 4 - o, j)]
+        return remote(block, block, to_ring2(kind, o))
+
+    own_src = {0: tokens, 1: cotangent}
+    gathered = {0: g_tok, 1: g_cot}
+    one, two, three = {}, {}, {}
+
+    def start_own(k):
+        one[k, 0] = gather_ring1(gathered[k], 0, own_src[k])
+        two[k, 0, 0] = gather_ring2(gathered[k], 0, 0, own_src[k])
+
+    def start_other(k):
         own_copies[k].wait()
         g0[k].wait_recv()
-        g1.append(gather_one(gathered[k]))
-    arrived(g1[0])
-    x2 = gather_two(g_tok)
+        one[k, 1] = gather_ring1(gathered[k], 1)
+        two[k, 1, 0] = gather_ring2(gathered[k], 1, 0)
+
+    def ring2_send(k, kind, j):
+        one[k, kind][4 - j].wait_recv()
+        two[k, kind, j] = gather_ring2(gathered[k], kind, j)
+
+    def forward(k, kind, j, o):
+        two[k, kind, j][o].wait_recv()
+        three[k, kind, j, o] = gather_forward(gathered[k], kind, j, o)
+
+    FORWARDS = ((0, 1), (1, 3), (3, 1), (2, 3))
+
+    def gathered_near(k):
+        for kind in range(2):
+            for j in (0, 1, 3, 2):
+                for o in (1, 3):
+                    if (j, o) not in FORWARDS:
+                        two[k, kind, j][o].wait_recv()
+
+    def gathered_far(k):
+        for kind in range(2):
+            for j, o in FORWARDS:
+                three[k, kind, j, o].wait_recv()
+
+    g0 = [remote(tokens, g_tok.at[place(0, 0, 0)], x_partner)]
+    start_own(0)
+    g0.append(remote(cotangent, g_cot.at[place(0, 0, 0)], x_partner))
+    weight_in = remote(w_in, wi.at[:, pl.ds(hid, hid)], core_partner)
+    weight_out = remote(w_out, wo.at[pl.ds(hid, hid)], core_partner)
+    start_other(0)
+    one[1, 0] = gather_ring1(g_cot, 0, cotangent)
 
     tile = 256
     n_hid = 2 * hid // tile
@@ -216,15 +237,18 @@
             lax.fori_loop(0, slab // 16, body, 0)
 
     wide = 512
-    n_wide = feat // wide
     low_rows, high_rows = slice(0, 2 * rows), slice(2 * rows, 4 * rows)
 
-    def project(k, s):
+    def span(f):
+        return pl.ds(f[0] * (feat // f[1]), feat // f[1])
+
+    def project(k, s, f):
         chunk = rows_of((act, dpre)[k], OFFSETS[s])
         o = OFFSETS[s]
+        n = feat // f[1] // wide
 
         def body(t, _):
-            cols = pl.ds(pl.multiple_of(t * wide, wide), wide)
+            cols = pl.ds(pl.multiple_of((f[0] * n + t) * wide, wide), wide)
             value = nn(chunk, wo[:, cols]) if k == 0 else nt(chunk, wi[cols, :])
             for h in range(2):
                 part = value[h * slab:(h + 1) * slab]
@@ -240,70 +264,82 @@
                     acc[k, h, :, cols] = part
             return 0
 
-        lax.fori_loop(0, n_wide, body, 0)
-
-    def scatter_far(k):
-        copies = []
+        lax.fori_loop(0, n, body, 0)
+
+    far, near, merged, second, third = {}, {}, {}, {}, {}
+
+    def scatter_far(k, f):
+        project(k, 3, f)
+        cols = span(f)
+        far[k, f] = []
         for h in range(2):
-            copies.append(remote(q2.at[k, h, low_rows], r2.at[k, h, 0], ring2[h][1]))
-            copies.append(remote(q2.at[k, h, high_rows], r2.at[k, h, 1], ring2[h][3]))
-        return copies
-
-    def scatter_near(k, side):
+            for side, part in enumerate((low_rows, high_rows)):
+                far[k, f].append(remote(
+                    q2.at[k, h, part, cols], r2.at[k, h, side, :, cols], ring2[h][(1, 3)[side]]
+                ))
+
+    def scatter_near(k, f, side):
+        project(k, 1 + side, f)
         part = (high_rows, low_rows)[side]
-        return [
-            remote(s1.at[k, h, side, part], r1.at[k, h, side, part], ring2[h][(1, 3)[side]])
+        cols = span(f)
+        near.setdefault((k, f), []).extend(
+            remote(s1.at[k, h, side, part, cols], r1.at[k, h, side, part, cols], ring2[h][(1, 3)[side]])
             for h in range(2)
-        ]
-
-    def scatter_merge(k, far):
-        copies = []
+        )
+
+    def scatter_merge(k, f):
+        cols = span(f)
+        merged[k, f] = []
         for h in range(2):
             for side in range(2):
-                far[2 * h + side].wait_recv()
+                far[k, f][2 * h + side].wait_recv()
                 base = side * 2 * rows
 
                 def body(t, _):
                     r_in = pl.ds(pl.multiple_of(t * 16, 16), 16)
                     r_out = pl.ds(pl.multiple_of(base + t * 16, 16), 16)
-                    total = mid[k, h, side, r_in, :] + r2[k, h, side, r_in, :].astype(F32)
-                    s1[k, h, side, r_out, :] = total.astype(BF16)
+                    total = mid[k, h, side, r_in, cols] + r2[k, h, side, r_in, cols].astype(F32)
+                    s1[k, h, side, r_out, cols] = total.astype(BF16)
                     return 0
 
                 lax.fori_loop(0, 2 * rows // 16, body, 0)
                 part = (low_rows, high_rows)[side]
-                copies.append(
-                    remote(s1.at[k, h, side, part], r1.at[k, h, side, part], ring2[h][(1, 3)[side]])
-                )
-        return copies
-
-    def scatter_two(k, near, merged):
-        arrived(near)
-        arrived(merged)
-        copies = []
+                merged[k, f].append(remote(
+                    s1.at[k, h, side, part, cols], r1.at[k, h, side, part, cols],
+                    ring2[h][(1, 3)[side]],
+                ))
+
+    def scatter_two(k, f):
+        cols = span(f)
+        arrived(near[k, f])
+        arrived(merged[k, f])
+        second[k, f] = []
         for h in range(2):
-            for slot, o in enumerate((1, 3, 2)):
+            for slot, o in enumerate((2, 1, 3)):
                 r_in = piece(lax.rem(sub[h] + o, 4))
-                total = acc[k, h, r_in, :] + r1[k, h, 0, r_in, :].astype(F32)
-                u2[k, h, slot] = (total + r1[k, h, 1, r_in, :].astype(F32)).astype(BF16)
-                copies.append(remote(u2.at[k, h, slot], v2.at[k, h, slot], ring1[h][o]))
-        return copies
-
-    def scatter_three(k, copies):
-        arrived(copies)
+                total = acc[k, h, r_in, cols] + r1[k, h, 0, r_in, cols].astype(F32)
+                u2[k, h, slot, :, cols] = (total + r1[k, h, 1, r_in, cols].astype(F32)).astype(BF16)
+                second[k, f].append(remote(
+                    u2.at[k, h, slot, :, cols], v2.at[k, h, slot, :, cols], ring1[h][o]
+                ))
+
+    def scatter_three(k, f):
+        cols = span(f)
+        arrived(second[k, f])
         for h in range(2):
             r_in = piece(sub[h])
-            total = acc[k, h, r_in, :] + r1[k, h, 0, r_in, :].astype(F32)
-            total += r1[k, h, 1, r_in, :].astype(F32)
+            total = acc[k, h, r_in, cols] + r1[k, h, 0, r_in, cols].astype(F32)
+            total += r1[k, h, 1, r_in, cols].astype(F32)
             for slot in range(3):
-                total += v2[k, h, slot].astype(F32)
-            fin[k, h] = total
-        s3[k] = fin[k, 1 - low].astype(BF16)
-        return remote(s3.at[k], r3.at[k], x_partner)
-
-    def finish(k, copy):
-        copy.wait_recv()
-        (out, gin)[k][...] = (fin[k, low] + r3[k].astype(F32)).astype(BF16)
+                total += v2[k, h, slot, :, cols].astype(F32)
+            fin[k, h, :, cols] = total
+        s3[k, :, cols] = fin[k, 1 - low, :, cols].astype(BF16)
+        third[k, f] = remote(s3.at[k, :, cols], r3.at[k, :, cols], x_partner)
+
+    def finish(k, f):
+        cols = span(f)
+        third[k, f].wait_recv()
+        (out, gin)[k][:, cols] = (fin[k, low, :, cols] + r3[k, :, cols].astype(F32)).astype(BF16)
 
     mine, other = pl.ds(0, hid), pl.ds(hid, hid)
     tokens_all = 8 * slab
@@ -334,70 +370,102 @@
 
         lax.fori_loop(start, stop, body, 0)
 
+    forward(0, 0, 0, 1)
+    ring2_send(0, 0, 1)
+    ring2_send(0, 0, 3)
+    ring2_send(0, 0, 2)
+    ring2_send(0, 1, 1)
+    ring2_send(0, 1, 3)
+    ring2_send(0, 1, 2)
+    forward(0, 1, 0, 1)
     weight_copies[0].wait()
     weight_in.wait_recv()
-    p = [pre_step(0)]
-    arrived(x2[0])
-    x3 = gather_three(g_tok)
-    arrived(g1[1])
-    c2 = gather_two(g_cot)
-    arrived(x2[1])
-    p.append(pre_step(1))
-    p.append(pre_step(2))
-    arrived(x3)
-    p.append(pre_step(3))
+    p = {0: pre_step(0)}
+    forward(0, 0, 1, 3)
+    forward(0, 1, 1, 3)
+    forward(0, 0, 3, 1)
+    forward(0, 0, 2, 3)
+    own_copies[1].wait()
+    g0[1].wait_recv()
+    one[1, 1] = gather_ring1(g_cot, 1)
+    forward(0, 1, 3, 1)
+    forward(0, 1, 2, 3)
+    two[1, 0, 0] = gather_ring2(g_cot, 0, 0)
+    two[1, 1, 0] = gather_ring2(g_cot, 1, 0)
+    ring2_send(1, 0, 1)
+    ring2_send(1, 0, 3)
+    ring2_send(1, 0, 2)
+    gathered_near(0)
+    p[1] = pre_step(1)
+    gathered_far(0)
+    p[3] = pre_step(3)
+    p[2] = pre_step(2)
     every_tok = remote(g_tok, e_tok, core_partner)
+    forward(1, 0, 0, 1)
+    ring2_send(1, 1, 1)
+    ring2_send(1, 1, 3)
+    ring2_send(1, 1, 2)
+    forward(1, 1, 0, 1)
     weight_copies[1].wait()
     weight_out.wait_recv()
-    q = [dact_step(0)]
+    q = {0: dact_step(0)}
     act_step(0, p[0])
-    arrived(c2[0])
-    c3 = gather_three(g_cot)
+    forward(1, 0, 1, 3)
+    forward(1, 1, 1, 3)
+    forward(1, 0, 3, 1)
+    forward(1, 1, 3, 1)
+    forward(1, 0, 2, 3)
     act_step(1, p[1])
+    act_step(3, p[3])
+    forward(1, 1, 2, 3)
+    whole, first, last = (0, 1), (0, 2), (1, 2)
+    scatter_far(0, whole)
+    scatter_near(0, whole, 0)
+    gathered_near(1)
+    gathered_far(1)
+    q[3] = dact_step(3)
     act_step(2, p[2])
-    act_step(3, p[3])
-    project(0, 3)
-    far0 = scatter_far(0)
-    project(0, 1)
-    near0 = scatter_near(0, 0)
-    project(0, 2)
-    near0 += scatter_near(0, 1)
+    scatter_near(0, whole, 1)
     every_act = remote(act.at[:, :, :, other], e_act, core_partner)
-    arrived(c2[1])
-    arrived(c3)
-    q += [None, None, dact_step(3)]
     q[1] = dact_step(1)
+    scatter_merge(0, whole)
     q[2] = dact_step(2)
-    merged0 = scatter_merge(0, far0)
     every_cot = remote(g_cot, e_cot, core_partner)
     dpre_step(3, q[3])
-    project(1, 3)
-    far1 = scatter_far(1)
+    scatter_far(1, first)
+    scatter_far(1, last)
+    project(0, 0, whole)
     dpre_step(1, q[1])
-    project(1, 1)
-    near1 = scatter_near(1, 0)
+    scatter_near(1, first, 0)
+    scatter_two(0, whole)
+    scatter_near(1, last, 0)
     dpre_step(2, q[2])
-    project(1, 2)
-    near1 += scatter_near(1, 1)
-    project(0, 0)
-    two0 = scatter_two(0, near0, merged0)
+    scatter_near(1, first, 1)
+    scatter_merge(1, first)
+    scatter_near(1, last, 1)
+    scatter_merge(1, last)
     dpre_step(0, q[0])
     every_dpre = remote(dpre.at[:, :, :, other], e_dpre, core_partner)
-    merged1 = scatter_merge(1, far1)
-    project(1, 0)
+    project(1, 0, whole)
     every_act.wait_recv()
     turn_act()
-    three0 = scatter_three(0, two0)
     every_cot.wait_recv()
-    grad_out_part(0, feat // tile)
-    finish(0, three0)
-    two1 = scatter_two(1, near1, merged1)
+    grad_out_part(0, 4)
+    scatter_three(0, whole)
+    grad_out_part(4, 8)
+    scatter_two(1, first)
+    grad_out_part(8, 12)
+    finish(0, whole)
+    scatter_two(1, last)
     every_tok.wait_recv()
     every_dpre.wait_recv()
-    grad_in_part(0, feat // tile // 2)
-    three1 = scatter_three(1, two1)
-    grad_in_part(feat // tile // 2, feat // tile)
-    finish(1, three1)
+    grad_in_part(0, 4)
+    scatter_three(1, first)
+    grad_in_part(4, 8)
+    scatter_three(1, last)
+    grad_in_part(8, 12)
+    finish(1, first)
+    finish(1, last)
     for copy in sent:
         copy.wait_send()
 

time: 96.5 us -> 92.2 us (0.955)
  Pallas kernels: 95.5 us -> 91.3 us
    pallas_call x1, Pallas kernels: 91.7 us -> 87.5 us  [exchange(): pl.pallas_call(kernel, out_shape=[pltpu.VMEM((rows, feat), BF16), pltpu.V...]
where the time goes in v3:
time: 92.2 us; the launch traced here: 92 us
  Pallas kernels  91.3 us (99%)
    pallas_call x1, Pallas kernels, exchange(): pl.pallas_call(kernel, out_shape=[pltpu.VMEM((rows, feat), BF16), pltpu.V...  87.5 us
    pallas_call x1, Pallas kernels, drain(): pl.pallas_call(drain_kernel, out_shape=[pltpu.HBM(a.shape, a.dtype) for a...  3.84 us

profile of v3, /device:TPU:0, one launch (start us, length us, event | category | flops | bytes accessed | tf_op | source)
XLA Modules:
  0.0 92.0 jit_solution(9436079598767708103)
XLA Ops:
  0.6 87.5 %exchange.1 = (bf16[16,3072]{1,0:T(8,128)(2,1)S(1)}, bf16[16,3072]{1,0:T(8,128)(2,1)S(1)}, f32[3072,384]{1,0:T(8,128)S(1)}, f32[384,3072]{1,0:T(8,128)S(1)}) custom-call(bf16[16,3072]{1,0:T(8,128)(2,1)} %tokens.1, bf16[3072,384]{1,0:T(8,128)(2,1)} %w_in.1, bf16[384,3072]{1,0:T(8,128)(2,1)} %w_out.1, bf16[16,3072]{1,0:T(8,128)(2,1)} %cotangent.1), custom_call_target="tpu_custom_call" | custom-call | tf_op jit(solution)/shard_map/exchange/pallas_call | solution.py:508
  88.1 3.8 %drain.1 = (bf16[16,3072]{1,0:T(8,128)(2,1)}, bf16[16,3072]{1,0:T(8,128)(2,1)}, f32[3072,384]{1,0:T(8,128)}, f32[384,3072]{1,0:T(8,128)}) custom-call(bf16[16,3072]{1,0:T(8,128)(2,1)S(1)} %get-tuple-element.8.refs_0_, bf16[16,3072]{1,0:T(8,128)(2,1)S(1)} %get-tuple-element.9.refs_1_, f32[3072,384]{1,0:T(8,128)S(1)} %get-tuple-element.10.refs_2_, ...), custom_call_target="tpu_custom_call" | custom-call | tf_op jit(solution)/shard_map/drain/pallas_call | solution.py:542

commit v4 on v3

--- a/solution.py
+++ b/solution.py
@@ -55,7 +55,7 @@
     own = (y, z)
     sub = (z, y)
 
-    counter, counter_local, sent = [0], [0], []
+    counter, counter_local, sent, seen = [0], [0], [], set()
 
     def remote(src, dst, device):
         i = counter[0]
@@ -96,7 +96,14 @@
 
     def arrived(copies):
         for copy in copies:
-            copy.wait_recv()
+            if id(copy) not in seen:
+                seen.add(id(copy))
+                copy.wait_recv()
+
+    def landed(copy):
+        if id(copy) not in seen:
+            seen.add(id(copy))
+            copy.wait()
 
     def half_of(kind):
         return low if kind == 0 else 1 - low
@@ -114,96 +121,90 @@
         h = half_of(kind)
         return at(dy=o * (1 - h), dz=o * h)
 
-    def gather_ring1(g, kind, src=None):
-        block = g.at[place(kind, 0, 0)]
-        return {o: remote(block if src is None else src, block, to_ring1(kind, o)) for o in (1, 3, 2)}
-
-    def gather_ring2(g, kind, j, src=None):
-        block = g.at[place(kind, 0, j)]
-        return {o: remote(block if src is None else src, block, to_ring2(kind, o)) for o in (1, 3)}
-
-    def gather_forward(g, kind, j, o):
-        block = g.at[place(kind, 4 - o, j)]
-        return remote(block, block, to_ring2(kind, o))
-
     own_src = {0: tokens, 1: cotangent}
     gathered = {0: g_tok, 1: g_cot}
-    one, two, three = {}, {}, {}
-
-    def start_own(k):
-        one[k, 0] = gather_ring1(gathered[k], 0, own_src[k])
-        two[k, 0, 0] = gather_ring2(gathered[k], 0, 0, own_src[k])
-
-    def start_other(k):
-        own_copies[k].wait()
-        g0[k].wait_recv()
-        one[k, 1] = gather_ring1(gathered[k], 1)
-        two[k, 1, 0] = gather_ring2(gathered[k], 1, 0)
+    g0, one, two, three = {}, {}, {}, {}
+    FORWARDS = ((0, 1), (1, 3), (3, 1), (2, 3))
+
+    def send_x(k):
+        g0[k] = remote(own_src[k], gathered[k].at[place(0, 0, 0)], x_partner)
+
+    def source(k, kind, block):
+        if kind == 0:
+            return own_src[k]
+        arrived([g0[k]])
+        return block
+
+    def ring1_send(k, kind):
+        block = gathered[k].at[place(kind, 0, 0)]
+        src = source(k, kind, block)
+        one[k, kind] = {o: remote(src, block, to_ring1(kind, o)) for o in (1, 3)}
+
+    def ring1_forward(k, kind):
+        for o in (1, 3):
+            arrived([one[k, kind][o]])
+            h, i, r = place(kind, 0, 4 - o)
+            block = gathered[k].at[h, i, r, pl.ds((o // 2) * (feat // 2), feat // 2)]
+            one[k, kind, o] = remote(block, block, to_ring1(kind, o))
 
     def ring2_send(k, kind, j):
-        one[k, kind][4 - j].wait_recv()
-        two[k, kind, j] = gather_ring2(gathered[k], kind, j)
+        block = gathered[k].at[place(kind, 0, j)]
+        src = block
+        if j == 0:
+            src = source(k, kind, block)
+        elif j == 2:
+            arrived([one[k, kind, 1], one[k, kind, 3]])
+        else:
+            arrived([one[k, kind][4 - j]])
+        two[k, kind, j] = {o: remote(src, block, to_ring2(kind, o)) for o in (1, 3)}
 
     def forward(k, kind, j, o):
-        two[k, kind, j][o].wait_recv()
-        three[k, kind, j, o] = gather_forward(gathered[k], kind, j, o)
-
-    FORWARDS = ((0, 1), (1, 3), (3, 1), (2, 3))
-
-    def gathered_near(k):
+        arrived([two[k, kind, j][o]])
+        block = gathered[k].at[place(kind, 4 - o, j)]
+        three[k, kind, j, o] = remote(block, block, to_ring2(kind, o))
+
+    def gathered_side(k, o):
         for kind in range(2):
-            for j in (0, 1, 3, 2):
-                for o in (1, 3):
-                    if (j, o) not in FORWARDS:
-                        two[k, kind, j][o].wait_recv()
+            for j in range(4):
+                if (j, o) not in FORWARDS:
+                    arrived([two[k, kind, j][o]])
 
     def gathered_far(k):
         for kind in range(2):
             for j, o in FORWARDS:
-                three[k, kind, j, o].wait_recv()
-
-    g0 = [remote(tokens, g_tok.at[place(0, 0, 0)], x_partner)]
-    start_own(0)
-    g0.append(remote(cotangent, g_cot.at[place(0, 0, 0)], x_partner))
-    weight_in = remote(w_in, wi.at[:, pl.ds(hid, hid)], core_partner)
-    weight_out = remote(w_out, wo.at[pl.ds(hid, hid)], core_partner)
-    start_other(0)
-    one[1, 0] = gather_ring1(g_cot, 0, cotangent)
-
-    tile = 256
-    n_hid = 2 * hid // tile
+                arrived([three[k, kind, j, o]])
+
+    for copy in own_copies:
+        landed(copy)
+
+    core, p, q = {}, {}, {}
+    tile = feat // 3
+
+    def send_weights():
+        core["w_in"] = remote(w_in, wi.at[:, pl.ds(hid, hid)], core_partner)
+        core["w_out"] = remote(w_out, wo.at[pl.ds(hid, hid)], core_partner)
 
     def rows_of(g, o):
         return jnp.concatenate([g[h, ring_at(h, o)] for h in range(2)], axis=0)
 
     def pre_step(s):
-        chunk = rows_of(g_tok, OFFSETS[s])
-
-        def body(t, _):
-            cols = pl.ds(pl.multiple_of(t * tile, tile), tile)
-            value = nn(chunk, wi[:, cols])
-            pre[s, :, cols] = value
-            s_pre[s, :, cols] = value.astype(BF16)
-            return 0
-
-        lax.fori_loop(0, n_hid, body, 0)
-        return remote(s_pre.at[s], r_pre.at[s], row_partner)
+        landed(weight_copies[0])
+        arrived([core["w_in"]])
+        value = nn(rows_of(g_tok, OFFSETS[s]), wi[...])
+        pre[s] = value
+        s_pre[s] = value.astype(BF16)
+        p[s] = remote(s_pre.at[s], r_pre.at[s], row_partner)
 
     def dact_step(s):
-        chunk = rows_of(g_cot, OFFSETS[s])
-
-        def body(t, _):
-            cols = pl.ds(pl.multiple_of(t * tile, tile), tile)
-            value = nt(chunk, wo[cols, :])
-            dact[s, :, cols] = value
-            s_dact[s, :, cols] = value.astype(BF16)
-            return 0
-
-        lax.fori_loop(0, n_hid, body, 0)
-        return remote(s_dact.at[s], r_dact.at[s], row_partner)
-
-    def act_step(s, copy):
-        copy.wait_recv()
+        landed(weight_copies[1])
+        arrived([core["w_out"]])
+        value = nt(rows_of(g_cot, OFFSETS[s]), wo[...])
+        dact[s] = value
+        s_dact[s] = value.astype(BF16)
+        q[s] = remote(s_dact.at[s], r_dact.at[s], row_partner)
+
+    def act_step(s):
+        arrived([p[s]])
         for h in range(2):
             i = ring_at(h, OFFSETS[s])
 
@@ -222,8 +223,8 @@
 
             lax.fori_loop(0, slab // 16, body, 0)
 
-    def dpre_step(s, copy):
-        copy.wait_recv()
+    def dpre_step(s):
+        arrived([q[s]])
         for h in range(2):
             i = ring_at(h, OFFSETS[s])
 
@@ -236,35 +237,30 @@
 
             lax.fori_loop(0, slab // 16, body, 0)
 
-    wide = 512
     low_rows, high_rows = slice(0, 2 * rows), slice(2 * rows, 4 * rows)
 
     def span(f):
-        return pl.ds(f[0] * (feat // f[1]), feat // f[1])
+        return pl.ds(f[0] * (feat // 6), f[1] * (feat // 6))
 
     def project(k, s, f):
         chunk = rows_of((act, dpre)[k], OFFSETS[s])
         o = OFFSETS[s]
-        n = feat // f[1] // wide
-
-        def body(t, _):
-            cols = pl.ds(pl.multiple_of((f[0] * n + t) * wide, wide), wide)
-            value = nn(chunk, wo[:, cols]) if k == 0 else nt(chunk, wi[cols, :])
-            for h in range(2):
-                part = value[h * slab:(h + 1) * slab]
-                if o == 2:
-                    q2[k, h, :, cols] = part.astype(BF16)
-                elif o == 1:
-                    s1[k, h, 0, high_rows, cols] = part[high_rows].astype(BF16)
-                    mid[k, h, 0, :, cols] = part[low_rows]
-                elif o == 3:
-                    s1[k, h, 1, low_rows, cols] = part[low_rows].astype(BF16)
-                    mid[k, h, 1, :, cols] = part[high_rows]
-                else:
-                    acc[k, h, :, cols] = part
-            return 0
-
-        lax.fori_loop(0, n, body, 0)
+        cols = span(f)
+        landed(weight_copies[k - 1])
+        arrived([core[("w_out", "w_in")[k]]])
+        value = nn(chunk, wo[:, cols]) if k == 0 else nt(chunk, wi[cols, :])
+        for h in range(2):
+            part = value[h * slab:(h + 1) * slab]
+            if o == 2:
+                q2[k, h, :, cols] = part.astype(BF16)
+            elif o == 1:
+                s1[k, h, 0, high_rows, cols] = part[high_rows].astype(BF16)
+                mid[k, h, 0, :, cols] = part[low_rows]
+            elif o == 3:
+                s1[k, h, 1, low_rows, cols] = part[low_rows].astype(BF16)
+                mid[k, h, 1, :, cols] = part[high_rows]
+            else:
+                acc[k, h, :, cols] = part
 
     far, near, merged, second, third = {}, {}, {}, {}, {}
 
@@ -292,7 +288,7 @@
         merged[k, f] = []
         for h in range(2):
             for side in range(2):
-                far[k, f][2 * h + side].wait_recv()
+                arrived([far[k, f][2 * h + side]])
                 base = side * 2 * rows
 
                 def body(t, _):
@@ -338,7 +334,7 @@
 
     def finish(k, f):
         cols = span(f)
-        third[k, f].wait_recv()
+        arrived([third[k, f]])
         (out, gin)[k][:, cols] = (fin[k, low, :, cols] + r3[k, :, cols].astype(F32)).astype(BF16)
 
     mine, other = pl.ds(0, hid), pl.ds(hid, hid)
@@ -347,11 +343,23 @@
     def flat(value):
         return value.reshape(tokens_all, value.shape[-1])
 
+    def send_core(name):
+        src, dst = {
+            "tok": (g_tok, e_tok),
+            "cot": (g_cot, e_cot),
+            "act": (act.at[:, :, :, other], e_act),
+            "dpre": (dpre.at[:, :, :, other], e_dpre),
+        }[name]
+        core[name] = remote(src, dst, core_partner)
+
     def turn_act():
+        arrived([core["act"]])
         act_t[0] = jnp.transpose(flat(act[:, :, :, mine]))
         act_t[1] = jnp.transpose(flat(e_act[...]))
 
     def grad_out_part(start, stop):
+        arrived([core["cot"]])
+
         def body(t, _):
             cols = pl.ds(pl.multiple_of(t * tile, tile), tile)
             value = nn(act_t[0], flat(g_cot[:, :, :, cols]))
@@ -361,6 +369,8 @@
         lax.fori_loop(start, stop, body, 0)
 
     def grad_in_part(start, stop):
+        arrived([core["tok"], core["dpre"]])
+
         def body(t, _):
             cols = pl.ds(pl.multiple_of(t * tile, tile), tile)
             value = contract_rows(flat(g_tok[:, :, :, cols]), flat(dpre[:, :, :, mine]))
@@ -370,100 +380,104 @@
 
         lax.fori_loop(start, stop, body, 0)
 
+    whole, first, last = (0, 6), (0, 4), (4, 2)
+    send_x(0)
+    ring1_send(0, 0)
+    ring2_send(1, 0, 0)
+    ring1_send(1, 0)
+    send_weights()
+    ring2_send(0, 0, 0)
+    ring1_send(0, 1)
+    ring1_forward(0, 0)
+    ring2_send(0, 0, 1)
+    ring2_send(0, 1, 0)
+    ring1_forward(1, 0)
+    ring1_forward(0, 1)
+    ring2_send(0, 1, 3)
+    ring2_send(0, 0, 2)
+    ring2_send(0, 0, 3)
+    send_x(1)
+    ring2_send(0, 1, 1)
+    ring2_send(0, 1, 2)
+    ring1_send(1, 1)
+    pre_step(0)
     forward(0, 0, 0, 1)
-    ring2_send(0, 0, 1)
-    ring2_send(0, 0, 3)
-    ring2_send(0, 0, 2)
-    ring2_send(0, 1, 1)
-    ring2_send(0, 1, 3)
-    ring2_send(0, 1, 2)
+    forward(0, 0, 2, 3)
+    forward(0, 1, 1, 3)
+    forward(0, 1, 3, 1)
+    forward(0, 0, 1, 3)
     forward(0, 1, 0, 1)
-    weight_copies[0].wait()
-    weight_in.wait_recv()
-    p = {0: pre_step(0)}
-    forward(0, 0, 1, 3)
-    forward(0, 1, 1, 3)
     forward(0, 0, 3, 1)
-    forward(0, 0, 2, 3)
-    own_copies[1].wait()
-    g0[1].wait_recv()
-    one[1, 1] = gather_ring1(g_cot, 1)
-    forward(0, 1, 3, 1)
     forward(0, 1, 2, 3)
-    two[1, 0, 0] = gather_ring2(g_cot, 0, 0)
-    two[1, 1, 0] = gather_ring2(g_cot, 1, 0)
+    ring2_send(1, 1, 0)
+    gathered_side(0, 3)
+    gathered_side(0, 1)
+    pre_step(1)
+    ring1_forward(1, 1)
+    ring2_send(1, 1, 1)
+    ring2_send(1, 0, 3)
+    forward(1, 0, 0, 1)
+    gathered_far(0)
+    pre_step(3)
+    ring2_send(1, 1, 3)
+    send_core("tok")
+    ring2_send(1, 0, 2)
+    pre_step(2)
+    ring2_send(1, 1, 2)
+    forward(1, 0, 3, 1)
+    forward(1, 1, 0, 1)
     ring2_send(1, 0, 1)
-    ring2_send(1, 0, 3)
-    ring2_send(1, 0, 2)
-    gathered_near(0)
-    p[1] = pre_step(1)
-    gathered_far(0)
-    p[3] = pre_step(3)
-    p[2] = pre_step(2)
-    every_tok = remote(g_tok, e_tok, core_partner)
-    forward(1, 0, 0, 1)
-    ring2_send(1, 1, 1)
-    ring2_send(1, 1, 3)
-    ring2_send(1, 1, 2)
-    forward(1, 1, 0, 1)
-    weight_copies[1].wait()
-    weight_out.wait_recv()
-    q = {0: dact_step(0)}
-    act_step(0, p[0])
+    act_step(0)
+    act_step(1)
+    forward(1, 0, 2, 3)
+    forward(1, 1, 3, 1)
+    forward(1, 1, 1, 3)
+    project(0, 0, whole)
+    act_step(3)
+    forward(1, 1, 2, 3)
     forward(1, 0, 1, 3)
-    forward(1, 1, 1, 3)
-    forward(1, 0, 3, 1)
-    forward(1, 1, 3, 1)
-    forward(1, 0, 2, 3)
-    act_step(1, p[1])
-    act_step(3, p[3])
-    forward(1, 1, 2, 3)
-    whole, first, last = (0, 1), (0, 2), (1, 2)
     scatter_far(0, whole)
+    gathered_side(1, 3)
+    dact_step(1)
     scatter_near(0, whole, 0)
-    gathered_near(1)
+    act_step(2)
+    scatter_near(0, whole, 1)
     gathered_far(1)
-    q[3] = dact_step(3)
-    act_step(2, p[2])
-    scatter_near(0, whole, 1)
-    every_act = remote(act.at[:, :, :, other], e_act, core_partner)
-    q[1] = dact_step(1)
+    dact_step(3)
+    gathered_side(1, 1)
+    dact_step(2)
+    send_core("act")
     scatter_merge(0, whole)
-    q[2] = dact_step(2)
-    every_cot = remote(g_cot, e_cot, core_partner)
-    dpre_step(3, q[3])
+    send_core("cot")
+    dact_step(0)
+    dpre_step(3)
+    scatter_far(1, last)
     scatter_far(1, first)
-    scatter_far(1, last)
-    project(0, 0, whole)
-    dpre_step(1, q[1])
+    turn_act()
+    dpre_step(1)
+    scatter_two(0, whole)
     scatter_near(1, first, 0)
-    scatter_two(0, whole)
-    scatter_near(1, last, 0)
-    dpre_step(2, q[2])
+    dpre_step(2)
     scatter_near(1, first, 1)
     scatter_merge(1, first)
+    scatter_near(1, last, 0)
+    dpre_step(0)
     scatter_near(1, last, 1)
+    send_core("dpre")
     scatter_merge(1, last)
-    dpre_step(0, q[0])
-    every_dpre = remote(dpre.at[:, :, :, other], e_dpre, core_partner)
+    scatter_three(0, whole)
     project(1, 0, whole)
-    every_act.wait_recv()
-    turn_act()
-    every_cot.wait_recv()
-    grad_out_part(0, 4)
-    scatter_three(0, whole)
-    grad_out_part(4, 8)
+    grad_in_part(1, 2)
     scatter_two(1, first)
-    grad_out_part(8, 12)
+    grad_out_part(1, 2)
+    scatter_two(1, last)
+    grad_out_part(2, 3)
+    grad_out_part(0, 1)
     finish(0, whole)
-    scatter_two(1, last)
-    every_tok.wait_recv()
-    every_dpre.wait_recv()
-    grad_in_part(0, 4)
     scatter_three(1, first)
-    grad_in_part(4, 8)
     scatter_three(1, last)
-    grad_in_part(8, 12)
+    grad_in_part(2, 3)
+    grad_in_part(0, 1)
     finish(1, first)
     finish(1, last)
     for copy in sent:

time: 92.2 us -> 87.5 us (0.949)
  Pallas kernels: 91.3 us -> 86.6 us
    pallas_call x1, Pallas kernels: 87.5 us -> 82.7 us  [exchange(): pl.pallas_call(kernel, out_shape=[pltpu.VMEM((rows, feat), BF16), pltpu.V...]
where the time goes in v4:
time: 87.5 us; the launch traced here: 87.4 us
  Pallas kernels  86.6 us (99%)
    pallas_call x1, Pallas kernels, exchange(): pl.pallas_call(kernel, out_shape=[pltpu.VMEM((rows, feat), BF16), pltpu.V...  82.7 us
    pallas_call x1, Pallas kernels, drain(): pl.pallas_call(drain_kernel, out_shape=[pltpu.HBM(a.shape, a.dtype) for a...  3.84 us

profile of v4, /device:TPU:0, one launch (start us, length us, event | category | flops | bytes accessed | tf_op | source)
XLA Modules:
  0.0 87.4 jit_solution(1816548808219854846)
XLA Ops:
  0.6 82.7 %exchange.1 = (bf16[16,3072]{1,0:T(8,128)(2,1)S(1)}, bf16[16,3072]{1,0:T(8,128)(2,1)S(1)}, f32[3072,384]{1,0:T(8,128)S(1)}, f32[384,3072]{1,0:T(8,128)S(1)}) custom-call(bf16[16,3072]{1,0:T(8,128)(2,1)} %tokens.1, bf16[3072,384]{1,0:T(8,128)(2,1)} %w_in.1, bf16[384,3072]{1,0:T(8,128)(2,1)} %w_out.1, bf16[16,3072]{1,0:T(8,128)(2,1)} %cotangent.1), custom_call_target="tpu_custom_call" | custom-call | tf_op jit(solution)/shard_map/exchange/pallas_call | solution.py:522
  83.4 3.8 %drain.1 = (bf16[16,3072]{1,0:T(8,128)(2,1)}, bf16[16,3072]{1,0:T(8,128)(2,1)}, f32[3072,384]{1,0:T(8,128)}, f32[384,3072]{1,0:T(8,128)}) custom-call(bf16[16,3072]{1,0:T(8,128)(2,1)S(1)} %get-tuple-element.8.refs_0_, bf16[16,3072]{1,0:T(8,128)(2,1)S(1)} %get-tuple-element.9.refs_1_, f32[3072,384]{1,0:T(8,128)S(1)} %get-tuple-element.10.refs_2_, ...), custom_call_target="tpu_custom_call" | custom-call | tf_op jit(solution)/shard_map/drain/pallas_call | solution.py:556

commit v5 on v4

--- a/solution.py
+++ b/solution.py
@@ -10,7 +10,7 @@
 MESH = pl.DeviceIdType.MESH
 BF16, F32 = jnp.bfloat16, jnp.float32
 OFFSETS = (0, 1, 3, 2)
-N_REMOTE = 160
+N_REMOTE = 176
 N_LOCAL = 16
 
 
@@ -178,6 +178,7 @@
         landed(copy)
 
     core, p, q = {}, {}, {}
+    mine, other = pl.ds(0, hid), pl.ds(hid, hid)
     tile = feat // 3
 
     def send_weights():
@@ -190,21 +191,27 @@
     def pre_step(s):
         landed(weight_copies[0])
         arrived([core["w_in"]])
-        value = nn(rows_of(g_tok, OFFSETS[s]), wi[...])
-        pre[s] = value
-        s_pre[s] = value.astype(BF16)
-        p[s] = remote(s_pre.at[s], r_pre.at[s], row_partner)
+        chunk = rows_of(g_tok, OFFSETS[s])
+        p[s] = []
+        for part in (mine, other):
+            value = nn(chunk, wi[:, part])
+            pre[s, :, part] = value
+            s_pre[s, :, part] = value.astype(BF16)
+            p[s].append(remote(s_pre.at[s, :, part], r_pre.at[s, :, part], row_partner))
 
     def dact_step(s):
         landed(weight_copies[1])
         arrived([core["w_out"]])
-        value = nt(rows_of(g_cot, OFFSETS[s]), wo[...])
-        dact[s] = value
-        s_dact[s] = value.astype(BF16)
-        q[s] = remote(s_dact.at[s], r_dact.at[s], row_partner)
+        chunk = rows_of(g_cot, OFFSETS[s])
+        q[s] = []
+        for part in (mine, other):
+            value = nt(chunk, wo[part, :])
+            dact[s, :, part] = value
+            s_dact[s, :, part] = value.astype(BF16)
+            q[s].append(remote(s_dact.at[s, :, part], r_dact.at[s, :, part], row_partner))
 
     def act_step(s):
-        arrived([p[s]])
+        arrived(p[s])
         for h in range(2):
             i = ring_at(h, OFFSETS[s])
 
@@ -224,7 +231,7 @@
             lax.fori_loop(0, slab // 16, body, 0)
 
     def dpre_step(s):
-        arrived([q[s]])
+        arrived(q[s])
         for h in range(2):
             i = ring_at(h, OFFSETS[s])
 
@@ -262,6 +269,7 @@
             else:
                 acc[k, h, :, cols] = part
 
+    whole, first, last = (0, 6), (0, 4), (4, 2)
     far, near, merged, second, third = {}, {}, {}, {}, {}
 
     def scatter_far(k, f):
@@ -319,6 +327,37 @@
                     u2.at[k, h, slot, :, cols], v2.at[k, h, slot, :, cols], ring1[h][o]
                 ))
 
+    left_cols, right_cols = pl.ds(0, feat // 2), pl.ds(feat // 2, feat // 2)
+
+    def term(k, h, o, cols):
+        r_in = piece(lax.rem(sub[h] + o, 4))
+        total = acc[k, h, r_in, cols] + r1[k, h, 0, r_in, cols].astype(F32)
+        return total + r1[k, h, 1, r_in, cols].astype(F32)
+
+    def second_send(k, h, slot, cols, o):
+        return remote(u2.at[k, h, slot, :, cols], v2.at[k, h, slot, :, cols], ring1[h][o])
+
+    def scatter_two_start(k):
+        arrived(near[k, whole])
+        arrived(merged[k, whole])
+        second[k, whole] = []
+        for h in range(2):
+            for cols, o in ((left_cols, 1), (right_cols, 3)):
+                u2[k, h, 0, :, cols] = term(k, h, 2, cols).astype(BF16)
+                second[k, whole].append(second_send(k, h, 0, cols, o))
+            u2[k, h, 1, :, right_cols] = term(k, h, 1, right_cols).astype(BF16)
+            second[k, whole].append(second_send(k, h, 1, right_cols, 1))
+            u2[k, h, 2, :, left_cols] = term(k, h, 3, left_cols).astype(BF16)
+            second[k, whole].append(second_send(k, h, 2, left_cols, 3))
+
+    def scatter_two_merge(k):
+        for h in range(2):
+            for cols, o, slot in ((left_cols, 1, 1), (right_cols, 3, 2)):
+                arrived([second[k, whole][4 * h + slot - 1]])
+                total = term(k, h, o, cols) + v2[k, h, 0, :, cols].astype(F32)
+                u2[k, h, slot, :, cols] = total.astype(BF16)
+                second[k, whole].append(second_send(k, h, slot, cols, o))
+
     def scatter_three(k, f):
         cols = span(f)
         arrived(second[k, f])
@@ -326,7 +365,7 @@
             r_in = piece(sub[h])
             total = acc[k, h, r_in, cols] + r1[k, h, 0, r_in, cols].astype(F32)
             total += r1[k, h, 1, r_in, cols].astype(F32)
-            for slot in range(3):
+            for slot in range(1 - k, 3):
                 total += v2[k, h, slot, :, cols].astype(F32)
             fin[k, h, :, cols] = total
         s3[k, :, cols] = fin[k, 1 - low, :, cols].astype(BF16)
@@ -337,7 +376,6 @@
         arrived([third[k, f]])
         (out, gin)[k][:, cols] = (fin[k, low, :, cols] + r3[k, :, cols].astype(F32)).astype(BF16)
 
-    mine, other = pl.ds(0, hid), pl.ds(hid, hid)
     tokens_all = 8 * slab
 
     def flat(value):
@@ -380,105 +418,105 @@
 
         lax.fori_loop(start, stop, body, 0)
 
-    whole, first, last = (0, 6), (0, 4), (4, 2)
     send_x(0)
     ring1_send(0, 0)
-    ring2_send(1, 0, 0)
+    ring2_send(0, 0, 0)
     ring1_send(1, 0)
     send_weights()
-    ring2_send(0, 0, 0)
+    ring2_send(1, 0, 0)
     ring1_send(0, 1)
     ring1_forward(0, 0)
+    ring2_send(0, 1, 0)
     ring2_send(0, 0, 1)
-    ring2_send(0, 1, 0)
+    send_x(1)
     ring1_forward(1, 0)
     ring1_forward(0, 1)
+    ring2_send(0, 0, 3)
+    ring2_send(0, 1, 1)
+    ring2_send(0, 0, 2)
     ring2_send(0, 1, 3)
-    ring2_send(0, 0, 2)
-    ring2_send(0, 0, 3)
-    send_x(1)
-    ring2_send(0, 1, 1)
+    forward(0, 0, 0, 1)
+    ring1_send(1, 1)
     ring2_send(0, 1, 2)
-    ring1_send(1, 1)
+    forward(0, 0, 1, 3)
     pre_step(0)
-    forward(0, 0, 0, 1)
+    forward(0, 1, 0, 1)
+    forward(0, 1, 1, 3)
+    forward(0, 0, 3, 1)
+    forward(0, 1, 3, 1)
+    gathered_side(0, 1)
+    forward(0, 1, 2, 3)
     forward(0, 0, 2, 3)
-    forward(0, 1, 1, 3)
-    forward(0, 1, 3, 1)
-    forward(0, 0, 1, 3)
-    forward(0, 1, 0, 1)
-    forward(0, 0, 3, 1)
-    forward(0, 1, 2, 3)
     ring2_send(1, 1, 0)
     gathered_side(0, 3)
-    gathered_side(0, 1)
-    pre_step(1)
+    ring2_send(1, 0, 1)
+    pre_step(2)
+    ring2_send(1, 1, 3)
+    ring2_send(1, 1, 1)
     ring1_forward(1, 1)
-    ring2_send(1, 1, 1)
-    ring2_send(1, 0, 3)
-    forward(1, 0, 0, 1)
+    ring2_send(1, 0, 2)
     gathered_far(0)
     pre_step(3)
-    ring2_send(1, 1, 3)
+    pre_step(1)
+    ring2_send(1, 0, 3)
+    ring2_send(1, 1, 2)
     send_core("tok")
-    ring2_send(1, 0, 2)
-    pre_step(2)
-    ring2_send(1, 1, 2)
+    forward(1, 0, 1, 3)
+    forward(1, 0, 0, 1)
+    act_step(0)
+    forward(1, 1, 1, 3)
+    act_step(2)
+    forward(1, 1, 0, 1)
+    forward(1, 1, 3, 1)
+    project(0, 0, whole)
+    forward(1, 1, 2, 3)
+    forward(1, 0, 2, 3)
     forward(1, 0, 3, 1)
-    forward(1, 1, 0, 1)
-    ring2_send(1, 0, 1)
-    act_step(0)
-    act_step(1)
-    forward(1, 0, 2, 3)
-    forward(1, 1, 3, 1)
-    forward(1, 1, 1, 3)
-    project(0, 0, whole)
     act_step(3)
-    forward(1, 1, 2, 3)
-    forward(1, 0, 1, 3)
     scatter_far(0, whole)
     gathered_side(1, 3)
+    gathered_side(1, 1)
     dact_step(1)
-    scatter_near(0, whole, 0)
-    act_step(2)
     scatter_near(0, whole, 1)
     gathered_far(1)
+    act_step(1)
+    scatter_near(0, whole, 0)
     dact_step(3)
-    gathered_side(1, 1)
+    send_core("act")
     dact_step(2)
-    send_core("act")
+    send_core("cot")
     scatter_merge(0, whole)
-    send_core("cot")
     dact_step(0)
+    dpre_step(1)
+    scatter_near(1, last, 0)
     dpre_step(3)
     scatter_far(1, last)
     scatter_far(1, first)
-    turn_act()
-    dpre_step(1)
-    scatter_two(0, whole)
     scatter_near(1, first, 0)
+    scatter_two_start(0)
     dpre_step(2)
+    scatter_near(1, last, 1)
     scatter_near(1, first, 1)
     scatter_merge(1, first)
-    scatter_near(1, last, 0)
     dpre_step(0)
-    scatter_near(1, last, 1)
     send_core("dpre")
     scatter_merge(1, last)
+    project(1, 0, whole)
+    turn_act()
+    scatter_two_merge(0)
+    grad_out_part(0, 1)
+    scatter_two(1, first)
+    grad_in_part(1, 2)
+    scatter_two(1, last)
     scatter_three(0, whole)
-    project(1, 0, whole)
-    grad_in_part(1, 2)
-    scatter_two(1, first)
     grad_out_part(1, 2)
-    scatter_two(1, last)
+    grad_in_part(2, 3)
+    scatter_three(1, first)
     grad_out_part(2, 3)
-    grad_out_part(0, 1)
-    finish(0, whole)
-    scatter_three(1, first)
     scatter_three(1, last)
-    grad_in_part(2, 3)
     grad_in_part(0, 1)
     finish(1, first)
+    finish(0, whole)
     finish(1, last)
     for copy in sent:
         copy.wait_send()

time: 87.5 us -> 86.8 us (level)
  no operation moved by 1% of the time
where the time goes in v5:
time: 86.8 us; the launch traced here: 86.7 us
  Pallas kernels  85.9 us (99%)
    pallas_call x1, Pallas kernels, exchange(): pl.pallas_call(kernel, out_shape=[pltpu.VMEM((rows, feat), BF16), pltpu.V...  82.1 us
    pallas_call x1, Pallas kernels, drain(): pl.pallas_call(drain_kernel, out_shape=[pltpu.HBM(a.shape, a.dtype) for a...  3.84 us

profile of v5, /device:TPU:0, one launch (start us, length us, event | category | flops | bytes accessed | tf_op | source)
XLA Modules:
  0.0 86.7 jit_solution(6876564494023372581)
XLA Ops:
  0.6 82.1 %exchange.1 = (bf16[16,3072]{1,0:T(8,128)(2,1)S(1)}, bf16[16,3072]{1,0:T(8,128)(2,1)S(1)}, f32[3072,384]{1,0:T(8,128)S(1)}, f32[384,3072]{1,0:T(8,128)S(1)}) custom-call(bf16[16,3072]{1,0:T(8,128)(2,1)} %tokens.1, bf16[3072,384]{1,0:T(8,128)(2,1)} %w_in.1, bf16[384,3072]{1,0:T(8,128)(2,1)} %w_out.1, bf16[16,3072]{1,0:T(8,128)(2,1)} %cotangent.1), custom_call_target="tpu_custom_call" | custom-call | tf_op jit(solution)/shard_map/exchange/pallas_call | solution.py:560
  82.7 3.8 %drain.1 = (bf16[16,3072]{1,0:T(8,128)(2,1)}, bf16[16,3072]{1,0:T(8,128)(2,1)}, f32[3072,384]{1,0:T(8,128)}, f32[384,3072]{1,0:T(8,128)}) custom-call(bf16[16,3072]{1,0:T(8,128)(2,1)S(1)} %get-tuple-element.8.refs_0_, bf16[16,3072]{1,0:T(8,128)(2,1)S(1)} %get-tuple-element.9.refs_1_, f32[3072,384]{1,0:T(8,128)S(1)} %get-tuple-element.10.refs_2_, ...), custom_call_target="tpu_custom_call" | custom-call | tf_op jit(solution)/shard_map/drain/pallas_call | solution.py:594

commit v6 on v5

--- a/solution.py
+++ b/solution.py
@@ -10,7 +10,7 @@
 MESH = pl.DeviceIdType.MESH
 BF16, F32 = jnp.bfloat16, jnp.float32
 OFFSETS = (0, 1, 3, 2)
-N_REMOTE = 176
+N_REMOTE = 208
 N_LOCAL = 16
 
 
@@ -123,7 +123,7 @@
 
     own_src = {0: tokens, 1: cotangent}
     gathered = {0: g_tok, 1: g_cot}
-    g0, one, two, three = {}, {}, {}, {}
+    g0, one, two, three, swapped = {}, {}, {}, {}, {}
     FORWARDS = ((0, 1), (1, 3), (3, 1), (2, 3))
 
     def send_x(k):
@@ -135,17 +135,32 @@
         arrived([g0[k]])
         return block
 
+    def columns(k, kind):
+        return (0, feat) if k == 0 else (kind * (feat // 2), feat // 2)
+
     def ring1_send(k, kind):
         block = gathered[k].at[place(kind, 0, 0)]
         src = source(k, kind, block)
-        one[k, kind] = {o: remote(src, block, to_ring1(kind, o)) for o in (1, 3)}
+        start, size = columns(k, kind)
+        cols = pl.ds(start, size)
+        one[k, kind] = {
+            o: remote(src.at[:, cols], block.at[:, cols], to_ring1(kind, o)) for o in (1, 3)
+        }
 
     def ring1_forward(k, kind):
         for o in (1, 3):
             arrived([one[k, kind][o]])
             h, i, r = place(kind, 0, 4 - o)
-            block = gathered[k].at[h, i, r, pl.ds((o // 2) * (feat // 2), feat // 2)]
+            start, size = columns(k, kind)
+            block = gathered[k].at[h, i, r, pl.ds(start + (o // 2) * (size // 2), size // 2)]
             one[k, kind, o] = remote(block, block, to_ring1(kind, o))
+
+    def swap(kind, j):
+        arrived([one[1, kind, 1], one[1, kind, 3]] if j == 2 else [one[1, kind][4 - j]])
+        h, i, r = place(kind, 0, j)
+        start, size = columns(1, kind)
+        block = g_cot.at[h, i, r, pl.ds(start, size)]
+        swapped[kind, j] = remote(block, block, x_partner)
 
     def ring2_send(k, kind, j):
         block = gathered[k].at[place(kind, 0, j)]
@@ -156,6 +171,8 @@
             arrived([one[k, kind, 1], one[k, kind, 3]])
         else:
             arrived([one[k, kind][4 - j]])
+        if k == 1 and j > 0:
+            arrived([swapped[1 - kind, j]])
         two[k, kind, j] = {o: remote(src, block, to_ring2(kind, o)) for o in (1, 3)}
 
     def forward(k, kind, j, o):
@@ -269,7 +286,7 @@
             else:
                 acc[k, h, :, cols] = part
 
-    whole, first, last = (0, 6), (0, 4), (4, 2)
+    whole = (0, 6)
     far, near, merged, second, third = {}, {}, {}, {}, {}
 
     def scatter_far(k, f):
@@ -419,105 +436,118 @@
         lax.fori_loop(start, stop, body, 0)
 
     send_x(0)
-    ring1_send(0, 0)
+    send_weights()
     ring2_send(0, 0, 0)
     ring1_send(1, 0)
-    send_weights()
+    ring1_send(0, 0)
     ring2_send(1, 0, 0)
+    send_x(1)
+    ring1_forward(1, 0)
+    swap(0, 1)
+    ring2_send(0, 1, 0)
+    swap(0, 3)
     ring1_send(0, 1)
     ring1_forward(0, 0)
-    ring2_send(0, 1, 0)
+    swap(0, 2)
+    ring1_send(1, 1)
+    ring2_send(1, 1, 0)
     ring2_send(0, 0, 1)
-    send_x(1)
-    ring1_forward(1, 0)
+    ring2_send(0, 1, 1)
     ring1_forward(0, 1)
+    ring2_send(0, 1, 3)
+    swap(1, 1)
+    forward(0, 1, 0, 1)
+    ring1_forward(1, 1)
     ring2_send(0, 0, 3)
-    ring2_send(0, 1, 1)
+    swap(1, 3)
+    forward(0, 0, 0, 1)
     ring2_send(0, 0, 2)
-    ring2_send(0, 1, 3)
-    forward(0, 0, 0, 1)
-    ring1_send(1, 1)
+    swap(1, 2)
     ring2_send(0, 1, 2)
+    pre_step(0)
+    forward(0, 1, 1, 3)
+    forward(0, 1, 3, 1)
     forward(0, 0, 1, 3)
-    pre_step(0)
-    forward(0, 1, 0, 1)
-    forward(0, 1, 1, 3)
     forward(0, 0, 3, 1)
-    forward(0, 1, 3, 1)
-    gathered_side(0, 1)
+    forward(0, 0, 2, 3)
     forward(0, 1, 2, 3)
-    forward(0, 0, 2, 3)
-    ring2_send(1, 1, 0)
+    ring2_send(1, 0, 1)
+    ring2_send(1, 1, 1)
+    ring2_send(1, 0, 3)
+    ring2_send(1, 1, 3)
     gathered_side(0, 3)
-    ring2_send(1, 0, 1)
-    pre_step(2)
-    ring2_send(1, 1, 3)
-    ring2_send(1, 1, 1)
-    ring1_forward(1, 1)
-    ring2_send(1, 0, 2)
+    ring2_send(1, 1, 2)
+    pre_step(1)
+    act_step(0)
     gathered_far(0)
     pre_step(3)
-    pre_step(1)
-    ring2_send(1, 0, 3)
-    ring2_send(1, 1, 2)
+    ring2_send(1, 0, 2)
+    gathered_side(0, 1)
+    forward(1, 0, 0, 1)
+    pre_step(2)
+    forward(1, 1, 0, 1)
+    project(0, 0, whole)
+    forward(1, 0, 1, 3)
+    forward(1, 1, 1, 3)
     send_core("tok")
-    forward(1, 0, 1, 3)
-    forward(1, 0, 0, 1)
-    act_step(0)
-    forward(1, 1, 1, 3)
-    act_step(2)
-    forward(1, 1, 0, 1)
     forward(1, 1, 3, 1)
-    project(0, 0, whole)
+    forward(1, 0, 3, 1)
+    forward(1, 0, 2, 3)
+    gathered_side(1, 1)
     forward(1, 1, 2, 3)
-    forward(1, 0, 2, 3)
-    forward(1, 0, 3, 1)
+    act_step(1)
     act_step(3)
     scatter_far(0, whole)
     gathered_side(1, 3)
-    gathered_side(1, 1)
-    dact_step(1)
+    dact_step(2)
+    gathered_far(1)
+    scatter_near(0, whole, 0)
+    act_step(2)
     scatter_near(0, whole, 1)
-    gathered_far(1)
-    act_step(1)
-    scatter_near(0, whole, 0)
     dact_step(3)
-    send_core("act")
-    dact_step(2)
     send_core("cot")
     scatter_merge(0, whole)
+    dact_step(1)
+    dpre_step(2)
     dact_step(0)
+    scatter_near(1, (3, 2), 1)
+    dpre_step(3)
+    scatter_far(1, (5, 1))
+    scatter_far(1, (3, 2))
+    scatter_near(1, (5, 1), 1)
+    scatter_far(1, (0, 3))
+    scatter_two_start(0)
+    scatter_near(1, (0, 3), 1)
     dpre_step(1)
-    scatter_near(1, last, 0)
-    dpre_step(3)
-    scatter_far(1, last)
-    scatter_far(1, first)
-    scatter_near(1, first, 0)
-    scatter_two_start(0)
-    dpre_step(2)
-    scatter_near(1, last, 1)
-    scatter_near(1, first, 1)
-    scatter_merge(1, first)
+    scatter_near(1, (0, 3), 0)
+    send_core("act")
+    scatter_near(1, (3, 2), 0)
     dpre_step(0)
+    scatter_merge(1, (0, 3))
     send_core("dpre")
-    scatter_merge(1, last)
+    scatter_near(1, (5, 1), 0)
+    scatter_two_merge(0)
+    scatter_merge(1, (3, 2))
+    scatter_merge(1, (5, 1))
+    turn_act()
     project(1, 0, whole)
-    turn_act()
-    scatter_two_merge(0)
+    grad_out_part(1, 2)
+    scatter_two(1, (0, 3))
+    grad_in_part(2, 3)
+    scatter_three(0, whole)
+    grad_out_part(2, 3)
+    scatter_two(1, (3, 2))
+    scatter_two(1, (5, 1))
     grad_out_part(0, 1)
-    scatter_two(1, first)
+    grad_in_part(0, 1)
+    scatter_three(1, (0, 3))
+    finish(0, whole)
+    scatter_three(1, (3, 2))
+    scatter_three(1, (5, 1))
     grad_in_part(1, 2)
-    scatter_two(1, last)
-    scatter_three(0, whole)
-    grad_out_part(1, 2)
-    grad_in_part(2, 3)
-    scatter_three(1, first)
-    grad_out_part(2, 3)
-    scatter_three(1, last)
-    grad_in_part(0, 1)
-    finish(1, first)
-    finish(0, whole)
-    finish(1, last)
+    finish(1, (0, 3))
+    finish(1, (3, 2))
+    finish(1, (5, 1))
     for copy in sent:
         copy.wait_send()
 

time: 86.8 us -> 86 us (level)
  no operation moved by 1% of the time
where the time goes in v6:
time: 86 us; the launch traced here: 85.9 us
  Pallas kernels  85.1 us (99%)
    pallas_call x1, Pallas kernels, exchange(): pl.pallas_call(kernel, out_shape=[pltpu.VMEM((rows, feat), BF16), pltpu.V...  81.2 us
    pallas_call x1, Pallas kernels, drain(): pl.pallas_call(drain_kernel, out_shape=[pltpu.HBM(a.shape, a.dtype) for a...  3.84 us

profile of v6, /device:TPU:0, one launch (start us, length us, event | category | flops | bytes accessed | tf_op | source)
XLA Modules:
  0.0 85.9 jit_solution(7325891468476020738)
XLA Ops:
  0.6 81.2 %exchange.1 = (bf16[16,3072]{1,0:T(8,128)(2,1)S(1)}, bf16[16,3072]{1,0:T(8,128)(2,1)S(1)}, f32[3072,384]{1,0:T(8,128)S(1)}, f32[384,3072]{1,0:T(8,128)S(1)}) custom-call(bf16[16,3072]{1,0:T(8,128)(2,1)} %tokens.1, bf16[3072,384]{1,0:T(8,128)(2,1)} %w_in.1, bf16[384,3072]{1,0:T(8,128)(2,1)} %w_out.1, bf16[16,3072]{1,0:T(8,128)(2,1)} %cotangent.1), custom_call_target="tpu_custom_call" | custom-call | tf_op jit(solution)/shard_map/exchange/pallas_call | solution.py:590
  81.9 3.8 %drain.1 = (bf16[16,3072]{1,0:T(8,128)(2,1)}, bf16[16,3072]{1,0:T(8,128)(2,1)}, f32[3072,384]{1,0:T(8,128)}, f32[384,3072]{1,0:T(8,128)}) custom-call(bf16[16,3072]{1,0:T(8,128)(2,1)S(1)} %get-tuple-element.8.refs_0_, bf16[16,3072]{1,0:T(8,128)(2,1)S(1)} %get-tuple-element.9.refs_1_, f32[3072,384]{1,0:T(8,128)S(1)} %get-tuple-element.10.refs_2_, ...), custom_call_target="tpu_custom_call" | custom-call | tf_op jit(solution)/shard_map/drain/pallas_call | solution.py:624

commit v7 on v6

--- a/solution.py
+++ b/solution.py
@@ -290,14 +290,15 @@
     far, near, merged, second, third = {}, {}, {}, {}, {}
 
     def scatter_far(k, f):
-        project(k, 3, f)
-        cols = span(f)
-        far[k, f] = []
-        for h in range(2):
-            for side, part in enumerate((low_rows, high_rows)):
-                far[k, f].append(remote(
-                    q2.at[k, h, part, cols], r2.at[k, h, side, :, cols], ring2[h][(1, 3)[side]]
-                ))
+        far[k, f] = [[] for _ in range(4)]
+        for g in ((0, 3), (3, 3)) if k == 0 else (f,):
+            project(k, 3, g)
+            cols = span(g)
+            for h in range(2):
+                for side, part in enumerate((low_rows, high_rows)):
+                    far[k, f][2 * h + side].append(remote(
+                        q2.at[k, h, part, cols], r2.at[k, h, side, :, cols], ring2[h][(1, 3)[side]]
+                    ))
 
     def scatter_near(k, f, side):
         project(k, 1 + side, f)
@@ -313,7 +314,7 @@
         merged[k, f] = []
         for h in range(2):
             for side in range(2):
-                arrived([far[k, f][2 * h + side]])
+                arrived(far[k, f][2 * h + side])
                 base = side * 2 * rows
 
                 def body(t, _):

time: 86 us -> 86.1 us (level)
  no operation moved by 1% of the time
where the time goes in v7:
time: 86.1 us; the launch traced here: 86 us
  Pallas kernels  85.2 us (99%)
    pallas_call x1, Pallas kernels, exchange(): pl.pallas_call(kernel, out_shape=[pltpu.VMEM((rows, feat), BF16), pltpu.V...  81.3 us
    pallas_call x1, Pallas kernels, drain(): pl.pallas_call(drain_kernel, out_shape=[pltpu.HBM(a.shape, a.dtype) for a...  3.84 us

profile of v7, /device:TPU:0, one launch (start us, length us, event | category | flops | bytes accessed | tf_op | source)
XLA Modules:
  0.0 86.0 jit_solution(361437548700205444)
XLA Ops:
  0.6 81.3 %exchange.1 = (bf16[16,3072]{1,0:T(8,128)(2,1)S(1)}, bf16[16,3072]{1,0:T(8,128)(2,1)S(1)}, f32[3072,384]{1,0:T(8,128)S(1)}, f32[384,3072]{1,0:T(8,128)S(1)}) custom-call(bf16[16,3072]{1,0:T(8,128)(2,1)} %tokens.1, bf16[3072,384]{1,0:T(8,128)(2,1)} %w_in.1, bf16[384,3072]{1,0:T(8,128)(2,1)} %w_out.1, bf16[16,3072]{1,0:T(8,128)(2,1)} %cotangent.1), custom_call_target="tpu_custom_call" | custom-call | tf_op jit(solution)/shard_map/exchange/pallas_call | solution.py:591
  82.0 3.8 %drain.1 = (bf16[16,3072]{1,0:T(8,128)(2,1)}, bf16[16,3072]{1,0:T(8,128)(2,1)}, f32[3072,384]{1,0:T(8,128)}, f32[384,3072]{1,0:T(8,128)}) custom-call(bf16[16,3072]{1,0:T(8,128)(2,1)S(1)} %get-tuple-element.8.refs_0_, bf16[16,3072]{1,0:T(8,128)(2,1)S(1)} %get-tuple-element.9.refs_1_, f32[3072,384]{1,0:T(8,128)S(1)} %get-tuple-element.10.refs_2_, ...), custom_call_target="tpu_custom_call" | custom-call | tf_op jit(solution)/shard_map/drain/pallas_call | solution.py:625
